TPU v7x, 32 devices: a whole 2x2x4 slice. The times are simulated.
32 devices in a mesh: dp: 8 (over z, x), tensor: 4 (over y, core).
Axes of the slice: x: 2, y: 2, z: 4, core: 2. Of those that a mesh axis runs over, the one named last changes fastest.
Arguments:
- layer_input: bfloat16 [8, 1032, 1024], P('dp', 'tensor'), may hold values from -6 to 6
- query_weight: bfloat16 [1024, 1024], P('dp', 'tensor'), may hold values from -0.1875 to 0.1875
- key_weight: bfloat16 [1024, 1024], P('dp', 'tensor'), may hold values from -0.1875 to 0.1875
- value_weight: bfloat16 [1024, 1024], P('dp', 'tensor'), may hold values from -0.1875 to 0.1875
- query_bias: bfloat16 [1024], P('dp'), may hold values from -3 to 3
- value_bias: bfloat16 [1024], P('dp'), may hold values from -3 to 3
- first_gain: bfloat16 [1024], P('dp'), may hold values from 0.099609375 to 1.8984375
- first_bias: bfloat16 [1024], P('dp'), may hold values from -3 to 3
- mixer_gain: bfloat16 [1024], P('dp'), may hold values from 0.099609375 to 1.8984375
- mixer_bias: bfloat16 [1024], P('dp'), may hold values from -3 to 3
- output_weight: bfloat16 [1024, 1024], P('tensor', 'dp'), may hold values from -0.1875 to 0.1875
- output_bias: bfloat16 [1024], P('dp'), may hold values from -3 to 3
- second_gain: bfloat16 [1024], P('dp'), may hold values from 0.099609375 to 1.8984375
- second_bias: bfloat16 [1024], P('dp'), may hold values from -3 to 3
- gate_weight: bfloat16 [1024, 2736], P('dp', 'tensor'), may hold values from -0.1875 to 0.1875
- up_weight: bfloat16 [1024, 2736], P('dp', 'tensor'), may hold values from -0.1875 to 0.1875
- gate_bias: bfloat16 [2736], P('tensor'), may hold values from -3 to 3
- up_bias: bfloat16 [2736], P('tensor'), may hold values from -3 to 3
- inner_gain: bfloat16 [2736], P('tensor'), may hold values from 0.099609375 to 1.8984375
- inner_bias: bfloat16 [2736], P('tensor'), may hold values from -3 to 3
- down_weight: bfloat16 [2736, 1024], P('tensor', 'dp'), may hold values from -0.109375 to 0.109375
- down_bias: bfloat16 [1024], P('dp'), may hold values from -3 to 3
- cotangent: bfloat16 [8, 1032, 1024], P('dp', 'tensor'), may hold values from -6 to 6
- key_valid: int32 [8, 1032], P('dp'), may hold values from 0 to 1, as said below
- patch_row: int32 [8, 1032], P('dp'), may hold values from 0 to 31
- patch_column: int32 [8, 1032], P('dp'), may hold values from 0 to 31
Outputs:
- layer_output: bfloat16 [8, 1032, 1024], P('dp', 'tensor')
- input_grad: float32 [8, 1032, 1024], P('dp', 'tensor')
- query_weight_grad: float32 [1024, 1024], P('dp', 'tensor')
- key_weight_grad: float32 [1024, 1024], P('dp', 'tensor')
- value_weight_grad: float32 [1024, 1024], P('dp', 'tensor')
- query_bias_grad: float32 [1024], P('dp')
- value_bias_grad: float32 [1024], P('dp')
- first_gain_grad: float32 [1024], P('dp')
- first_bias_grad: float32 [1024], P('dp')
- mixer_gain_grad: float32 [1024], P('dp')
- mixer_bias_grad: float32 [1024], P('dp')
- output_weight_grad: float32 [1024, 1024], P('tensor', 'dp')
- output_bias_grad: float32 [1024], P('dp')
- second_gain_grad: float32 [1024], P('dp')
- second_bias_grad: float32 [1024], P('dp')
- gate_weight_grad: float32 [1024, 2736], P('dp', 'tensor')
- up_weight_grad: float32 [1024, 2736], P('dp', 'tensor')
- gate_bias_grad: float32 [2736], P('tensor')
- up_bias_grad: float32 [2736], P('tensor')
- inner_gain_grad: float32 [2736], P('tensor')
- inner_bias_grad: float32 [2736], P('tensor')
- down_weight_grad: float32 [2736, 1024], P('tensor', 'dp')
- down_bias_grad: float32 [1024], P('dp')
Inputs may be any that keep to these rules, and one draw needn't show every extreme that they name: `key_valid`: slot 0 of every image, the class token, is a valid key.
All inputs are finite; a program needn't handle non-finite values.
Results may differ from a plain program's by a relative error of at most 0.015.
Values may be sent and summed in bfloat16 or wider, within the bound.
No kernel may reach another device: no remote copies, remote signals or barrier semaphores. Data moves between devices by JAX's collectives and lax.ppermute only.
A program may use at most 128 MiB of HBM per device.

v0:
```python
import math

import jax
import jax.numpy as jnp
from jax import lax
from jax.sharding import PartitionSpec as P

HD = 64


EPSILON = 1e-06


def normalize(values):
    center = jnp.mean(values, axis=-1, keepdims=True)
    spread = jnp.mean(values * values, axis=-1, keepdims=True) - center * center
    inverse = lax.rsqrt(spread + EPSILON)
    return ((values - center) * inverse, inverse)


def normalize_back(grad_hat, unit_hat, inverse):
    return inverse * (
        grad_hat
        - jnp.mean(grad_hat, axis=-1, keepdims=True)
        - unit_hat * jnp.mean(grad_hat * unit_hat, axis=-1, keepdims=True)
    )


def feature_sums(former, latter):
    first_total, second_total = lax.psum(
        (jnp.sum(former, axis=-1), jnp.sum(latter, axis=-1)), "tensor"
    )
    return (first_total[..., None], second_total[..., None])


def split_normalize(values):
    width_all = values.shape[-1] * lax.axis_size("tensor")
    summed, squared = feature_sums(values, values * values)
    center = summed / width_all
    spread = squared / width_all - center * center
    inverse = lax.rsqrt(spread + EPSILON)
    return ((values - center) * inverse, inverse)


def split_normalize_back(grad_hat, unit_hat, inverse):
    width_all = grad_hat.shape[-1] * lax.axis_size("tensor")
    summed, crossed = feature_sums(grad_hat, grad_hat * unit_hat)
    return inverse * (grad_hat - summed / width_all - unit_hat * (crossed / width_all))


def rotary_tables(patch_row, patch_column):
    quarter = HD // 4
    indices = jnp.arange(quarter).astype(jnp.float32)
    frequency = jnp.power(jnp.float32(10000.0), -indices / quarter)
    row_part = patch_row.astype(jnp.float32)[..., None] * frequency
    column_part = patch_column.astype(jnp.float32)[..., None] * frequency
    angles = 0.5 * jnp.concatenate([row_part, column_part], axis=-1)
    places = jnp.arange(patch_row.shape[-1])
    angles = jnp.where((places > 0)[:, None], angles, 0.0)
    return (jnp.cos(angles), jnp.sin(angles))


def rotate_pairs(values, cosine_table, sine_table):
    paired = values.reshape(values.shape[:-1] + (values.shape[-1] // 2, 2))
    even_part = paired[..., 0]
    odd_part = paired[..., 1]
    cosine_wide = cosine_table[..., None, :]
    sine_wide = sine_table[..., None, :]
    turned = jnp.stack(
        [
            even_part * cosine_wide - odd_part * sine_wide,
            even_part * sine_wide + odd_part * cosine_wide,
        ],
        axis=-1,
    )
    return turned.reshape(values.shape)


def to_items(values):
    return values.transpose(0, 2, 1, 3).reshape(-1, values.shape[1], values.shape[3])


def from_items(items, image_count):
    length = items.shape[1]
    shaped = items.reshape(image_count, -1, length, items.shape[2])
    return shaped.transpose(0, 2, 1, 3).reshape(image_count, length, -1)


def project(remaining_rows, weight_matrix):
    return jnp.einsum(
        "hno,ok->hnk", remaining_rows, weight_matrix, preferred_element_type=jnp.float32
    )


def project_back(gradient_row_block, weight_matrix):
    return jnp.einsum(
        "xhv,mv->xhm", gradient_row_block, weight_matrix, preferred_element_type=jnp.float32
    )


def outer_sum(remaining_rows, gradient_row_block):
    return jnp.einsum(
        "kcq,kct->qt", remaining_rows, gradient_row_block, preferred_element_type=jnp.float32
    )


def local_slice(vector, offset, count):
    return lax.dynamic_slice_in_dim(vector.astype(jnp.float32), offset, count)


def token_sum(values):
    return jnp.sum(values.astype(jnp.float32), axis=(0, 1))


def gather_rows(normed):
    return lax.all_gather(normed, "tensor", axis=1, tiled=True)


def scatter_rows(partial_rows):
    return lax.psum_scatter(partial_rows, "tensor", scatter_dimension=1, tiled=True)


def gather_grads(grads_low):
    return lax.all_gather(grads_low, "tensor", axis=1, tiled=True)


def scatter_grads(partial_rows):
    return lax.psum_scatter(partial_rows, "tensor", scatter_dimension=1, tiled=True)


def attention_set(
    query_weight,
    key_weight,
    value_weight,
    output_weight,
    query_bias,
    value_bias,
    first_gain,
    first_bias,
    mixer_gain,
    mixer_bias,
    output_bias,
):
    return (
        lax.all_gather(query_weight, "dp", axis=0, tiled=True),
        lax.all_gather(key_weight, "dp", axis=0, tiled=True),
        lax.all_gather(value_weight, "dp", axis=0, tiled=True),
        lax.all_gather(output_weight, "dp", axis=1, tiled=True),
        lax.all_gather(query_bias, "dp", axis=0, tiled=True),
        lax.all_gather(value_bias, "dp", axis=0, tiled=True),
        lax.all_gather(first_gain, "dp", axis=0, tiled=True),
        lax.all_gather(first_bias, "dp", axis=0, tiled=True),
        lax.all_gather(mixer_gain, "dp", axis=0, tiled=True),
        lax.all_gather(mixer_bias, "dp", axis=0, tiled=True),
        lax.all_gather(output_bias, "dp", axis=0, tiled=True),
    )


def feedforward_set(gate_weight, up_weight, down_weight, second_gain, second_bias, down_bias):
    return (
        lax.all_gather(gate_weight, "dp", axis=0, tiled=True),
        lax.all_gather(up_weight, "dp", axis=0, tiled=True),
        lax.all_gather(down_weight, "dp", axis=1, tiled=True),
        lax.all_gather(second_gain, "dp", axis=0, tiled=True),
        lax.all_gather(second_bias, "dp", axis=0, tiled=True),
        lax.all_gather(down_bias, "dp", axis=0, tiled=True),
    )


def attend_item(element):
    query_item, key_item, value_item, valid_item = element
    score_scale = 1.0 / math.sqrt(query_item.shape[-1])
    scores = (
        jnp.einsum("qd,kd->qk", query_item, key_item, preferred_element_type=jnp.float32)
        * score_scale
    )
    keep_mask = (valid_item == 1)[None, :]
    row_max = jnp.max(jnp.where(keep_mask, scores, -1e30), axis=-1, keepdims=True)
    exp_terms = jnp.where(keep_mask, jnp.exp(scores - row_max), 0.0)
    denominator = jnp.sum(exp_terms, axis=-1, keepdims=True)
    probabilities = (exp_terms / denominator).astype(jnp.bfloat16)
    attended = jnp.einsum(
        "qk,kd->qd", probabilities, value_item, preferred_element_type=jnp.float32
    )
    return (attended, (row_max + jnp.log(denominator))[:, 0])


def attend_back(element):
    query_item, key_item, value_item, valid_item, logsum_item, grad_item = element
    score_scale = 1.0 / math.sqrt(query_item.shape[-1])
    scores = (
        jnp.einsum("qd,kd->qk", query_item, key_item, preferred_element_type=jnp.float32)
        * score_scale
    )
    keep_mask = (valid_item == 1)[None, :]
    probabilities = jnp.where(keep_mask, jnp.exp(scores - logsum_item[:, None]), 0.0)
    probs_low = probabilities.astype(jnp.bfloat16)
    grad_value = jnp.einsum("qk,qd->kd", probs_low, grad_item, preferred_element_type=jnp.float32)
    grad_probs = jnp.einsum("qd,kd->qk", grad_item, value_item, preferred_element_type=jnp.float32)
    grad_scores = (
        probabilities * (grad_probs - jnp.sum(probabilities * grad_probs, axis=-1, keepdims=True))
    ).astype(jnp.bfloat16)
    grad_query = (
        jnp.einsum("qk,kd->qd", grad_scores, key_item, preferred_element_type=jnp.float32)
        * score_scale
    )
    grad_key = (
        jnp.einsum("qk,qd->kd", grad_scores, query_item, preferred_element_type=jnp.float32)
        * score_scale
    )
    return (grad_query, grad_key, grad_value)


def forward_pass(
    layer_input, weights_attn, weights_ffn, local_ffn, key_valid, cosine_table, sine_table, finish
):
    (
        query_full,
        key_full,
        value_full,
        complete_output,
        query_bias,
        value_bias,
        first_gain,
        first_bias,
        mixer_gain,
        mixer_bias,
        output_bias,
    ) = weights_attn
    gate_full, up_full, down_projection_whole, second_gain, second_bias, down_bias = weights_ffn
    gate_bias, up_bias, inner_gain, inner_bias = local_ffn
    head_width = query_full.shape[1]
    offset = lax.axis_index("tensor") * head_width
    residual = layer_input.astype(jnp.float32)
    unit_one, inverse_one = normalize(residual)
    normed_one = (
        unit_one * first_gain.astype(jnp.float32) + first_bias.astype(jnp.float32)
    ).astype(jnp.bfloat16)
    gathered_one = gather_rows(normed_one)
    image_count, length, model_width = gathered_one.shape
    head_count = head_width // HD
    split_shape = (image_count, length, head_count, HD)
    query_pre = project(gathered_one, query_full) + local_slice(query_bias, offset, head_width)
    key_pre = project(gathered_one, key_full)
    value_pre = project(gathered_one, value_full) + local_slice(value_bias, offset, head_width)
    queries = rotate_pairs(query_pre.reshape(split_shape), cosine_table, sine_table).astype(
        jnp.bfloat16
    )
    keys = rotate_pairs(key_pre.reshape(split_shape), cosine_table, sine_table).astype(jnp.bfloat16)
    values = value_pre.reshape(split_shape).astype(jnp.bfloat16)
    valid_items = jnp.repeat(key_valid, head_count, axis=0)
    attended_items, logsum = lax.map(
        attend_item, (to_items(queries), to_items(keys), to_items(values), valid_items)
    )
    attended = from_items(attended_items, image_count)
    unit_mix, inverse_mix = split_normalize(attended)
    mixer_result = (
        unit_mix * local_slice(mixer_gain, offset, head_width)
        + local_slice(mixer_bias, offset, head_width)
    ).astype(jnp.bfloat16)
    branch_one = scatter_rows(
        jnp.einsum("fvi,ir->fvr", mixer_result, complete_output, preferred_element_type=jnp.float32)
    ) + output_bias.astype(jnp.float32)
    hidden_state = residual + branch_one
    unit_two, inverse_two = normalize(hidden_state)
    normed_two = (
        unit_two * second_gain.astype(jnp.float32) + second_bias.astype(jnp.float32)
    ).astype(jnp.bfloat16)
    gathered_two = gather_rows(normed_two)
    gate_pre = project(gathered_two, gate_full) + gate_bias.astype(jnp.float32)
    up_pre = project(gathered_two, up_full) + up_bias.astype(jnp.float32)
    activated = jax.nn.silu(gate_pre) * up_pre
    unit_ffn, inverse_ffn = split_normalize(activated)
    inner_result = (
        unit_ffn * inner_gain.astype(jnp.float32) + inner_bias.astype(jnp.float32)
    ).astype(jnp.bfloat16)
    layer_out = layer_input
    if finish:
        branch_two = scatter_rows(
            jnp.einsum(
                "cah,ht->cat",
                inner_result,
                down_projection_whole,
                preferred_element_type=jnp.float32,
            )
        ) + down_bias.astype(jnp.float32)
        layer_out = (hidden_state + branch_two).astype(jnp.bfloat16)
    saved = {
        "unit_one": unit_one,
        "inverse_one": inverse_one,
        "gathered_one": gathered_one,
        "queries": queries,
        "keys": keys,
        "values": values,
        "valid_items": valid_items,
        "logsum": logsum,
        "unit_mix": unit_mix,
        "inverse_mix": inverse_mix,
        "mixed_out": mixer_result,
        "unit_two": unit_two,
        "inverse_two": inverse_two,
        "gathered_two": gathered_two,
        "gate_pre": gate_pre,
        "up_pre": up_pre,
        "unit_ffn": unit_ffn,
        "inverse_ffn": inverse_ffn,
        "inner_out": inner_result,
    }
    return (layer_out, saved)


def place_piece(piece, start, total_width):
    return lax.dynamic_update_slice_in_dim(jnp.zeros((total_width,), jnp.float32), piece, start, 0)


def local(
    layer_input,
    query_weight,
    key_weight,
    value_weight,
    query_bias,
    value_bias,
    first_gain,
    first_bias,
    mixer_gain,
    mixer_bias,
    output_weight,
    output_bias,
    second_gain,
    second_bias,
    gate_weight,
    up_weight,
    gate_bias,
    up_bias,
    inner_gain,
    inner_bias,
    down_weight,
    down_bias,
    cotangent,
    key_valid,
    patch_row,
    patch_column,
):
    cosine_table, sine_table = rotary_tables(patch_row, patch_column)
    local_ffn = (gate_bias, up_bias, inner_gain, inner_bias)
    weights_attn = attention_set(
        query_weight,
        key_weight,
        value_weight,
        output_weight,
        query_bias,
        value_bias,
        first_gain,
        first_bias,
        mixer_gain,
        mixer_bias,
        output_bias,
    )
    weights_ffn = feedforward_set(
        gate_weight, up_weight, down_weight, second_gain, second_bias, down_bias
    )
    layer_output, saved = forward_pass(
        layer_input, weights_attn, weights_ffn, local_ffn, key_valid, cosine_table, sine_table, True
    )
    weights_attn = attention_set(
        query_weight,
        key_weight,
        value_weight,
        output_weight,
        query_bias,
        value_bias,
        first_gain,
        first_bias,
        mixer_gain,
        mixer_bias,
        output_bias,
    )
    weights_ffn = feedforward_set(
        gate_weight, up_weight, down_weight, second_gain, second_bias, down_bias
    )
    saved = forward_pass(
        layer_input,
        weights_attn,
        weights_ffn,
        local_ffn,
        key_valid,
        cosine_table,
        sine_table,
        False,
    )[1]
    (
        query_full,
        key_full,
        value_full,
        complete_output,
        qbias_full,
        vbias_full,
        fgain_full,
        fbias_full,
        mgain_full,
        mbias_full,
        obias_full,
    ) = weights_attn
    gate_full, up_full, down_projection_whole, sgain_full, sbias_full, dbias_full = weights_ffn
    head_width = query_full.shape[1]
    offset = lax.axis_index("tensor") * head_width
    image_count = layer_input.shape[0]
    model_width = layer_input.shape[2]
    length = saved["gathered_one"].shape[1]
    split_shape = (image_count, length, head_width // HD, HD)
    grad_out = cotangent.astype(jnp.float32)
    gathered_grad = gather_grads(cotangent)
    down_bias_grad = token_sum(grad_out)
    down_weight_grad = outer_sum(saved["inner_out"], gathered_grad)
    grad_inner = project_back(gathered_grad, down_projection_whole)
    inner_gain_grad = token_sum(grad_inner * saved["unit_ffn"])
    inner_bias_grad = token_sum(grad_inner)
    grad_activated = split_normalize_back(
        grad_inner * inner_gain.astype(jnp.float32), saved["unit_ffn"], saved["inverse_ffn"]
    )
    gate_pre = saved["gate_pre"]
    sigmoid_gate = jax.nn.sigmoid(gate_pre)
    grad_gate = (
        grad_activated * saved["up_pre"] * sigmoid_gate * (1.0 + gate_pre * (1.0 - sigmoid_gate))
    ).astype(jnp.bfloat16)
    grad_up = (grad_activated * gate_pre * sigmoid_gate).astype(jnp.bfloat16)
    gate_bias_grad = token_sum(grad_gate)
    up_bias_grad = token_sum(grad_up)
    gate_weight_grad = outer_sum(saved["gathered_two"], grad_gate)
    up_weight_grad = outer_sum(saved["gathered_two"], grad_up)
    ffn_shards = (
        lax.psum_scatter(gate_weight_grad, "dp", scatter_dimension=0, tiled=True),
        lax.psum_scatter(up_weight_grad, "dp", scatter_dimension=0, tiled=True),
        lax.psum_scatter(down_weight_grad, "dp", scatter_dimension=1, tiled=True),
    )
    grad_second = scatter_grads(project_back(grad_gate, gate_full) + project_back(grad_up, up_full))
    second_gain_grad = token_sum(grad_second * saved["unit_two"])
    second_bias_grad = token_sum(grad_second)
    grad_hidden = grad_out + normalize_back(
        grad_second * sgain_full.astype(jnp.float32), saved["unit_two"], saved["inverse_two"]
    )
    branch_grad = grad_hidden.astype(jnp.bfloat16)
    output_bias_grad = token_sum(branch_grad)
    gathered_branch = gather_grads(branch_grad)
    output_weight_grad = outer_sum(saved["mixed_out"], gathered_branch)
    grad_mixed = project_back(gathered_branch, complete_output)
    mixer_gain_grad = token_sum(grad_mixed * saved["unit_mix"])
    mixer_bias_grad = token_sum(grad_mixed)
    grad_attended = split_normalize_back(
        grad_mixed * local_slice(mgain_full, offset, head_width),
        saved["unit_mix"],
        saved["inverse_mix"],
    ).astype(jnp.bfloat16)
    grad_query_items, grad_key_items, grad_value_items = lax.map(
        attend_back,
        (
            to_items(saved["queries"]),
            to_items(saved["keys"]),
            to_items(saved["values"]),
            saved["valid_items"],
            saved["logsum"],
            to_items(grad_attended.reshape(split_shape)),
        ),
    )
    grad_queries = from_items(grad_query_items, image_count).reshape(split_shape)
    grad_keys = from_items(grad_key_items, image_count).reshape(split_shape)
    grad_query_pre = (
        rotate_pairs(grad_queries, cosine_table, -sine_table)
        .reshape(image_count, length, head_width)
        .astype(jnp.bfloat16)
    )
    grad_key_pre = (
        rotate_pairs(grad_keys, cosine_table, -sine_table)
        .reshape(image_count, length, head_width)
        .astype(jnp.bfloat16)
    )
    grad_value_pre = from_items(grad_value_items, image_count).astype(jnp.bfloat16)
    query_bias_grad = token_sum(grad_query_pre)
    value_bias_grad = token_sum(grad_value_pre)
    query_weight_grad = outer_sum(saved["gathered_one"], grad_query_pre)
    key_weight_grad = outer_sum(saved["gathered_one"], grad_key_pre)
    value_weight_grad = outer_sum(saved["gathered_one"], grad_value_pre)
    attn_shards = (
        lax.psum_scatter(query_weight_grad, "dp", scatter_dimension=0, tiled=True),
        lax.psum_scatter(key_weight_grad, "dp", scatter_dimension=0, tiled=True),
        lax.psum_scatter(value_weight_grad, "dp", scatter_dimension=0, tiled=True),
        lax.psum_scatter(output_weight_grad, "dp", scatter_dimension=1, tiled=True),
    )
    grad_first = scatter_grads(
        project_back(grad_query_pre, query_full)
        + project_back(grad_key_pre, key_full)
        + project_back(grad_value_pre, value_full)
    )
    first_gain_grad = token_sum(grad_first * saved["unit_one"])
    first_bias_grad = token_sum(grad_first)
    input_grad = grad_hidden + normalize_back(
        grad_first * fgain_full.astype(jnp.float32), saved["unit_one"], saved["inverse_one"]
    )
    ffn_local = gate_bias.shape[0]
    ffn_offset = lax.axis_index("tensor") * ffn_local
    ffn_total = ffn_local * lax.axis_size("tensor")
    summed = lax.psum(
        (
            first_gain_grad,
            first_bias_grad,
            place_piece(query_bias_grad, offset, model_width),
            place_piece(value_bias_grad, offset, model_width),
            place_piece(mixer_gain_grad, offset, model_width),
            place_piece(mixer_bias_grad, offset, model_width),
            output_bias_grad,
            second_gain_grad,
            second_bias_grad,
            down_bias_grad,
            place_piece(gate_bias_grad, ffn_offset, ffn_total),
            place_piece(up_bias_grad, ffn_offset, ffn_total),
            place_piece(inner_gain_grad, ffn_offset, ffn_total),
            place_piece(inner_bias_grad, ffn_offset, ffn_total),
        ),
        ("dp", "tensor"),
    )
    dp_width = model_width // lax.axis_size("dp")
    dp_start = lax.axis_index("dp") * dp_width
    model_parts = [lax.dynamic_slice_in_dim(vector, dp_start, dp_width) for vector in summed[0:10]]
    ffn_parts = [
        lax.dynamic_slice_in_dim(vector, ffn_offset, ffn_local) for vector in summed[10:14]
    ]
    return (
        layer_output,
        input_grad,
        attn_shards[0],
        attn_shards[1],
        attn_shards[2],
        model_parts[2],
        model_parts[3],
        model_parts[0],
        model_parts[1],
        model_parts[4],
        model_parts[5],
        attn_shards[3],
        model_parts[6],
        model_parts[7],
        model_parts[8],
        ffn_shards[0],
        ffn_shards[1],
        ffn_parts[0],
        ffn_parts[1],
        ffn_parts[2],
        ffn_parts[3],
        ffn_shards[2],
        model_parts[9],
    )


def solution(mesh):
    in_specs = (
        P("dp", "tensor", None),
        P("dp", "tensor"),
        P("dp", "tensor"),
        P("dp", "tensor"),
        P("dp"),
        P("dp"),
        P("dp"),
        P("dp"),
        P("dp"),
        P("dp"),
        P("tensor", "dp"),
        P("dp"),
        P("dp"),
        P("dp"),
        P("dp", "tensor"),
        P("dp", "tensor"),
        P("tensor"),
        P("tensor"),
        P("tensor"),
        P("tensor"),
        P("tensor", "dp"),
        P("dp"),
        P("dp", "tensor", None),
        P("dp", None),
        P("dp", None),
        P("dp", None),
    )
    out_specs = (
        P("dp", "tensor", None),
        P("dp", "tensor", None),
        P("dp", "tensor"),
        P("dp", "tensor"),
        P("dp", "tensor"),
        P("dp"),
        P("dp"),
        P("dp"),
        P("dp"),
        P("dp"),
        P("dp"),
        P("tensor", "dp"),
        P("dp"),
        P("dp"),
        P("dp"),
        P("dp", "tensor"),
        P("dp", "tensor"),
        P("tensor"),
        P("tensor"),
        P("tensor"),
        P("tensor"),
        P("tensor", "dp"),
        P("dp"),
    )
    return jax.shard_map(local, mesh=mesh, in_specs=in_specs, out_specs=out_specs, check_vma=False)
```

profile of v0, /device:TPU:0, one launch (start us, length us, event | category | flops | bytes accessed | tf_op | source)
XLA Modules:
  0.0 1619.2 jit_solution(10006870345772856554)
XLA Ops:
  11.3 22.3 %all-gather = bf16[8,1,128]{2,1,0:T(2,128)(2,1)S(1)} all-gather(bf16[1,1,128]{2,1,0:T(2,128)(2,1)} %bitcast.311), channel_id=1, replica_groups=mesh['dp'=8,'tensor'=4] {'dp'}, dimensions={0}, use_global_device_ids=true | all-gather | bytes 2304 | tf_op jit(solution)/shard_map/all_gather | solution.py:151
  33.6 16.4 %all-gather.1 = bf16[8,1,128]{2,1,0:T(2,128)(2,1)S(1)} all-gather(bf16[1,1,128]{2,1,0:T(2,128)(2,1)} %bitcast.312), channel_id=1, replica_groups=mesh['dp'=8,'tensor'=4] {'dp'}, dimensions={0}, use_global_device_ids=true | all-gather | bytes 2304 | tf_op jit(solution)/shard_map/all_gather | solution.py:152
  54.5 18.1 %all-gather.2 = bf16[8,1,128]{2,1,0:T(2,128)(2,1)S(1)} all-gather(bf16[1,1,128]{2,1,0:T(2,128)(2,1)S(1)} %bitcast.313), channel_id=1, replica_groups=mesh['dp'=8,'tensor'=4] {'dp'}, dimensions={0}, use_global_device_ids=true | all-gather | bytes 2304 | tf_op jit(solution)/shard_map/all_gather | solution.py:149
  72.6 31.8 %all_gather.88 = bf16[1024,256]{1,0:T(8,128)(2,1)S(1)} all-gather(bf16[128,256]{1,0:T(8,128)(2,1)S(1)} %copy-done.36), channel_id=1, replica_groups=mesh['dp'=8,'tensor'=4] {'dp'}, dimensions={0}, use_global_device_ids=true | all-gather | bytes 589824 | tf_op jit(solution)/shard_map/all_gather | solution.py:146
  105.6 16.1 all-gather.3
  121.9 18.2 %all-gather.4 = bf16[8,1,128]{2,1,0:T(2,128)(2,1)S(1)} all-gather(bf16[1,1,128]{2,1,0:T(2,128)(2,1)S(1)} %bitcast.315), channel_id=1, replica_groups=mesh['dp'=8,'tensor'=4] {'dp'}, dimensions={0}, use_global_device_ids=true | all-gather | bytes 2304 | tf_op jit(solution)/shard_map/all_gather | solution.py:153
  140.2 16.2 all-gather.5
  156.5 31.5 %all_gather.86 = bf16[1024,256]{1,0:T(8,128)(2,1)S(1)} all-gather(bf16[128,256]{1,0:T(8,128)(2,1)S(1)} %copy-done.37), channel_id=1, replica_groups=mesh['dp'=8,'tensor'=4] {'dp'}, dimensions={0}, use_global_device_ids=true | all-gather | bytes 589824 | tf_op jit(solution)/shard_map/all_gather | solution.py:145
  188.0 31.6 %all_gather.89 = bf16[1024,256]{1,0:T(8,128)(2,1)S(1)} all-gather(bf16[128,256]{1,0:T(8,128)(2,1)S(1)} %copy-done.38), channel_id=1, replica_groups=mesh['dp'=8,'tensor'=4] {'dp'}, dimensions={0}, use_global_device_ids=true | all-gather | bytes 589824 | tf_op jit(solution)/shard_map/all_gather | solution.py:147
  219.6 28.3 %all_gather.93 = bf16[256,1024]{1,0:T(8,128)(2,1)} all-gather(bf16[256,128]{1,0:T(8,128)(2,1)S(1)} %copy-done.39), channel_id=1, replica_groups=mesh['dp'=8,'tensor'=4] {'dp'}, dimensions={1}, use_global_device_ids=true | all-gather | bytes 589824 | tf_op jit(solution)/shard_map/all_gather | solution.py:148
  270.6 27.1 %while.37 = (s32[]{:T(128)}, f32[4,1032,64]{1,2,0:T(8,128)S(1)}, f32[4,1032]{1,0:T(4,128)S(1)}, s32[4,1032]{1,0:T(4,128)S(1)}, bf16[4,1032,64]{2,1,0:T(8,128)(2,...) while((s32[]{:T(128)}, f32[4,1032,64]{1,2,0:T(8,128)S(1)}, ...), condition=%wide.region_21.22_spmd, body=%wide.region_18.21_spmd.sunk | while | flops 283296384 | bytes 31473648 | solution.py:252
  298.0 6.4 all-reduce.9
  307.8 8.4 copy.152
  319.3 16.5 %all-gather.6 = bf16[8,1,128]{2,1,0:T(2,128)(2,1)S(1)} all-gather(bf16[1,1,128]{2,1,0:T(2,128)(2,1)S(1)} %bitcast.317), channel_id=1, replica_groups=mesh['dp'=8,'tensor'=4] {'dp'}, dimensions={0}, use_global_device_ids=true | all-gather | bytes 2304 | tf_op jit(solution)/shard_map/all_gather | solution.py:155
  335.7 18.0 %all-gather.7 = bf16[8,1,128]{2,1,0:T(2,128)(2,1)S(1)} all-gather(bf16[1,1,128]{2,1,0:T(2,128)(2,1)S(1)} %bitcast.318), channel_id=1, replica_groups=mesh['dp'=8,'tensor'=4] {'dp'}, dimensions={0}, use_global_device_ids=true | all-gather | bytes 2304 | tf_op jit(solution)/shard_map/all_gather | solution.py:164
  353.7 16.5 %all-gather.8 = bf16[8,1,128]{2,1,0:T(2,128)(2,1)S(1)} all-gather(bf16[1,1,128]{2,1,0:T(2,128)(2,1)S(1)} %bitcast.319), channel_id=1, replica_groups=mesh['dp'=8,'tensor'=4] {'dp'}, dimensions={0}, use_global_device_ids=true | all-gather | bytes 2304 | tf_op jit(solution)/shard_map/all_gather | solution.py:165
  371.5 51.7 %all-reduce.17.cloned.1.call-done = f32[1,1032,1024]{2,0,1:T(1,128)} async-done(((f32[1,1032,1024]{2,0,1:T(1,128)}), f32[1,1032,1024]{2,0,1:T(1,128)}) %all-reduce.17.cloned.1.call-update) | async-done | bytes 4227088
  432.2 16.0 while.36
  448.3 7.0 fusion.140
  469.7 40.5 %all-gather.23.cloned.1.call-done = bf16[1024,684]{0,1:T(8,128)(2,1)} async-done(((bf16[128,684]{0,1:T(8,128)(2,1)}), bf16[1024,684]{0,1:T(8,128)(2,1)}) %all-gather.23.cloned.1.call-update) | async-done | bytes 1400848 | tf_op jit(solution)/shard_map/all_gather | solution.py:161
  510.2 5.7 convolution_add_fusion.4
  515.9 37.4 %all-gather.25.cloned.1.call-done = bf16[1024,684]{0,1:T(8,128)(2,1)} async-done(((bf16[128,684]{0,1:T(8,128)(2,1)}), bf16[1024,684]{0,1:T(8,128)(2,1)}) %all-gather.25.cloned.1.call-update) | async-done | bytes 1400848 | tf_op jit(solution)/shard_map/all_gather | solution.py:162
  553.3 8.1 multiply_reduce_fusion.3
  561.4 5.9 all-reduce.8
  571.4 11.3 all-reduce.7
  582.7 6.6 convert_reduce_fusion
  593.7 8.4 copy.157
  603.0 8.4 copy.145
  611.9 152.1 %all-reduce.23.cloned.1.call-done = (f32[1,1032,1024]{2,0,1:T(1,128)}, f32[1,1032,1024]{2,0,1:T(1,128)}) async-done(((f32[1,1032,1024]{2,0,1:T(1,128)}, f32[1,1032,1024]{2,0,1:T(1,128)}), (f32[1,1032,1024]{2,0,1:T(1,128)}, f32[1,1032,1024]{2,0,1:T(1,128)})) %all-reduce.23.cloned.1.call-update) | async-done | bytes 8454160
  768.3 6.7 multiply_reduce_fusion.6
  775.0 8.7 convert_reduce_fusion.4
  787.9 33.4 %all-gather.33.cloned.1.call-done = bf16[1,1032,1024]{2,0,1:T(2,128)(2,1)} async-done(((bf16[1,258,1024]{2,0,1:T(2,128)(2,1)}), bf16[1,1032,1024]{2,0,1:T(2,128)(2,1)}) %all-gather.33.cloned.1.call-update) | async-done | bytes 2113552 | tf_op jit(solution)/shard_map/all_gather | solution.py:124
  825.8 31.7 %all-gather.21.cloned.1.call-done = bf16[1,1032,1024]{2,0,1:T(2,128)(2,1)} async-done(((bf16[1,258,1024]{2,0,1:T(2,128)(2,1)}), bf16[1,1032,1024]{2,0,1:T(2,128)(2,1)}) %all-gather.21.cloned.1.call-update) | async-done | bytes 2113552 | tf_op jit(solution)/shard_map/all_gather | solution.py:116
  866.7 10.6 all-reduce.6
  882.0 34.2 %while.38 = (s32[]{:T(128)}, f32[4,1032,64]{1,2,0:T(8,128)}, f32[4,1032,64]{1,2,0:T(8,128)}, bf16[4,1032,64]{1,2,0:T(8,128)(2,1)}, s32[4,1032]{1,0:T(4,128)S(1)}...) while((s32[]{:T(128)}, f32[4,1032,64]{1,2,0:T(8,128)}, ...), condition=%wide.region_46.47_spmd, body=%wide.region_44.46_spmd.sunk | while | flops 691332672 | bytes 36208028 | solution.py:454
  928.2 8.4 copy.169
  938.8 8.5 copy.146
  951.8 150.8 %all-reduce.21.cloned.1.call-done = (f32[1,1032,1024]{2,0,1:T(1,128)}, f32[1,1032,1024]{2,0,1:T(1,128)}) async-done(((f32[1,1032,1024]{2,0,1:T(1,128)}, f32[1,1032,1024]{2,0,1:T(1,128)}), (f32[1,1032,1024]{2,0,1:T(1,128)}, f32[1,1032,1024]{2,0,1:T(1,128)})) %all-reduce.21.cloned.1.call-update) | async-done | bytes 8454160
  1102.6 6.3 multiply_reduce_fusion.8
  1109.0 5.8 fusion.70
  1121.5 5.2 fusion.74
  1140.0 20.6 %all-gather.9 = bf16[8,1,128]{2,1,0:T(2,128)(2,1)S(1)} all-gather(bf16[1,1,128]{2,1,0:T(2,128)(2,1)S(1)} %bitcast.320), channel_id=1, replica_groups=mesh['dp'=8,'tensor'=4] {'dp'}, dimensions={0}, use_global_device_ids=true | all-gather | bytes 2304 | tf_op jit(solution)/shard_map/all_gather | solution.py:166
  1169.0 94.8 %all-reduce.19.cloned.1.call-done = (f32[1024]{0:T(1024)}, f32[1024]{0:T(1024)}, f32[1024]{0:T(1024)}, f32[1024]{0:T(1024)}, f32[1024]{0:T(1024)}, /*index=5*/f3...) async-done(((f32[1024]{0:T(1024)}, f32[1024]{0:T(1024)}, ...) | async-done | bytes 84752 | tf_op jit(solution)/shard_map/psum | solution.py:502
  1281.9 62.4 %reduce-scatter.18.cloned.1.call-done = f32[128,684]{0,1:T(8,128)} async-done(((f32[1024,684]{0,1:T(8,128)}), f32[128,684]{0,1:T(8,128)}) %reduce-scatter.18.cloned.1.call-update) | async-done | bytes 350224 | tf_op jit(solution)/shard_map/reduce_scatter | solution.py:433
  1344.3 66.8 %reduce-scatter.14.cloned.1.call-done = f32[256,128]{1,0:T(8,128)} async-done(((f32[256,1024]{1,0:T(8,128)}), f32[256,128]{1,0:T(8,128)}) %reduce-scatter.14.cloned.1.call-update) | async-done | bytes 131088 | tf_op jit(solution)/shard_map/reduce_scatter | solution.py:487
  1411.1 66.8 %reduce-scatter.10.cloned.1.call-done = f32[128,256]{1,0:T(8,128)} async-done(((f32[1024,256]{1,0:T(8,128)}), f32[128,256]{1,0:T(8,128)}) %reduce-scatter.10.cloned.1.call-update) | async-done | bytes 131088 | tf_op jit(solution)/shard_map/reduce_scatter | solution.py:485
  1477.9 66.6 %reduce-scatter.8.cloned.1.call-done = f32[128,256]{1,0:T(8,128)} async-done(((f32[1024,256]{1,0:T(8,128)}), f32[128,256]{1,0:T(8,128)}) %reduce-scatter.8.cloned.1.call-update) | async-done | bytes 131088 | tf_op jit(solution)/shard_map/reduce_scatter | solution.py:484
  1544.4 66.7 %reduce-scatter.12.cloned.1.call-done = f32[128,256]{1,0:T(8,128)} async-done(((f32[1024,256]{1,0:T(8,128)}), f32[128,256]{1,0:T(8,128)}) %reduce-scatter.12.cloned.1.call-update) | async-done | bytes 131088 | tf_op jit(solution)/shard_map/reduce_scatter | solution.py:486
  (447 shorter events, 240.4 us)
Async XLA Ops:
  8.0 241.2 %all-gather.19.cloned.1.call-start = ((), (), s32[]{:S(2)}) async-start(), calls=%async_computation.7 | async-start | bytes 5283840 | tf_op jit(solution)/shard_map/all_gather | solution.py:116
  50.1 22.5 %copy-start.36 = (bf16[128,256]{1,0:T(8,128)(2,1)S(1)}, bf16[128,256]{1,0:T(8,128)(2,1)}, u32[]{:S(2)}) copy-start(bf16[128,256]{1,0:T(8,128)(2,1)} %param.34) | copy-start | bytes 196612
  54.4 51.2 %copy-start.61 = (bf16[128]{0:T(256)(128)(2,1)S(1)}, bf16[128]{0:T(256)(128)(2,1)}, u32[]{:S(2)}) copy-start(bf16[128]{0:T(256)(128)(2,1)} %param.37) | copy-start | bytes 772
  54.4 67.5 %copy-start.54 = (s32[1,1032]{1,0:T(1,128)S(1)}, s32[1,1032]{1,0:T(1,128)}, u32[]{:S(2)}) copy-start(s32[1,1032]{1,0:T(1,128)} %param.55) | copy-start | bytes 12388
  54.4 67.6 %copy-start.62 = (bf16[128]{0:T(256)(128)(2,1)S(1)}, bf16[128]{0:T(256)(128)(2,1)}, u32[]{:S(2)}) copy-start(bf16[128]{0:T(256)(128)(2,1)} %param.40) | copy-start | bytes 772
  54.4 85.8 %copy-start.63 = (bf16[128]{0:T(256)(128)(2,1)S(1)}, bf16[128]{0:T(256)(128)(2,1)}, u32[]{:S(2)}) copy-start(bf16[128]{0:T(256)(128)(2,1)} %param.41) | copy-start | bytes 772
  54.4 102.0 %copy-start.52 = (s32[1,1032]{1,0:T(1,128)S(1)}, s32[1,1032]{1,0:T(1,128)}, u32[]{:S(2)}) copy-start(s32[1,1032]{1,0:T(1,128)} %param.57) | copy-start | bytes 12388
  54.4 102.0 %copy-start.53 = (s32[1,1032]{1,0:T(1,128)S(1)}, s32[1,1032]{1,0:T(1,128)}, u32[]{:S(2)}) copy-start(s32[1,1032]{1,0:T(1,128)} %param.56) | copy-start | bytes 12388
  54.4 102.1 %copy-start.37 = (bf16[128,256]{1,0:T(8,128)(2,1)S(1)}, bf16[128,256]{1,0:T(8,128)(2,1)}, u32[]{:S(2)}) copy-start(bf16[128,256]{1,0:T(8,128)(2,1)} %param.33) | copy-start | bytes 196612
  54.4 368.8 %all-reduce.17.cloned.1.call-start = ((), (), s32[]{:S(2)}) async-start(), calls=%async_computation.22 | async-start | bytes 8454144
  72.6 115.4 %copy-start.38 = (bf16[128,256]{1,0:T(8,128)(2,1)S(1)}, bf16[128,256]{1,0:T(8,128)(2,1)}, u32[]{:S(2)}) copy-start(bf16[128,256]{1,0:T(8,128)(2,1)} %param.35) | copy-start | bytes 196612
  104.4 115.2 %copy-start.14 = (bf16[1024,256]{1,0:T(8,128)(2,1)}, bf16[1024,256]{1,0:T(8,128)(2,1)S(1)}, u32[]{:S(2)}) copy-start(bf16[1024,256]{1,0:T(8,128)(2,1)S(1)} %all_gather.88) | copy-start | bytes 1572868
  104.4 115.2 %copy-start.39 = (bf16[256,128]{1,0:T(8,128)(2,1)S(1)}, bf16[256,128]{1,0:T(8,128)(2,1)}, u32[]{:S(2)}) copy-start(bf16[256,128]{1,0:T(8,128)(2,1)} %param.42) | copy-start | bytes 196612
  188.0 64.3 %copy-start.29 = (bf16[1024,256]{1,0:T(8,128)(2,1)}, bf16[1024,256]{1,0:T(8,128)(2,1)S(1)}, u32[]{:S(2)}) copy-start(bf16[1024,256]{1,0:T(8,128)(2,1)S(1)} %all_gather.86) | copy-start | bytes 1572868
  219.6 45.2 %copy-start.27 = (bf16[1024,256]{1,0:T(8,128)(2,1)}, bf16[1024,256]{1,0:T(8,128)(2,1)S(1)}, u32[]{:S(2)}) copy-start(bf16[1024,256]{1,0:T(8,128)(2,1)S(1)} %all_gather.89) | copy-start | bytes 1572868
  316.3 37.4 %copy-start.66 = (bf16[128]{0:T(256)(128)(2,1)S(1)}, bf16[128]{0:T(256)(128)(2,1)}, u32[]{:S(2)}) copy-start(bf16[128]{0:T(256)(128)(2,1)} %param.45) | copy-start | bytes 772
  316.3 53.9 %copy-start.73 = (u32[32]{0:T(128)S(1)}, u32[32]{0:T(128)}, u32[]{:S(2)}) copy-start(u32[32]{0:T(128)} %constant.141) | copy-start | bytes 388
  316.4 106.9 %copy-start.12 = (bf16[1,258,1024]{2,1,0:T(8,128)(2,1)S(1)}, bf16[1,258,1024]{2,1,0:T(8,128)(2,1)}, u32[]{:S(2)}) copy-start(bf16[1,258,1024]{2,1,0:T(8,128)(2,1)} %param.32) | copy-start | bytes 1585156
  316.4 131.9 %all-gather.27.cloned.1.call-start = ((), (), s32[]{:S(2)}) async-start(), calls=%async_computation.11 | async-start | bytes 1585152 | tf_op jit(solution)/shard_map/all_gather | solution.py:163
  316.9 131.3 %all-gather.31.cloned.1.call-start = ((), (), s32[]{:S(2)}) async-start(), calls=%async_computation.13 | async-start | bytes 5283840 | tf_op jit(solution)/shard_map/all_gather | solution.py:124
  319.2 146.1 %all-gather.29.cloned.1.call-start = ((), (), s32[]{:S(2)}) async-start(), calls=%async_computation.12 | async-start | bytes 5283840 | tf_op jit(solution)/shard_map/all_gather | solution.py:116
  430.6 79.6 %all-gather.23.cloned.1.call-start = ((), (), s32[]{:S(2)}) async-start(), calls=%async_computation.9 | async-start | bytes 1585152 | tf_op jit(solution)/shard_map/all_gather | solution.py:161
  431.3 122.0 %all-gather.25.cloned.1.call-start = ((), (), s32[]{:S(2)}) async-start(), calls=%async_computation.10 | async-start | bytes 1585152 | tf_op jit(solution)/shard_map/all_gather | solution.py:162
  432.0 331.9 %all-reduce.23.cloned.1.call-start = ((), (), s32[]{:S(2)}) async-start(), calls=%async_computation.25 | async-start | bytes 16908288
  611.4 156.8 %copy-start.6 = (f32[1,258,1024]{2,0,1:T(1,128)S(1)}, f32[1,258,1024]{2,0,1:T(1,128)}, u32[]{:S(2)}) copy-start(f32[1,258,1024]{2,0,1:T(1,128)} %get-tuple-element.428) | copy-start | bytes 3170308
  611.4 209.9 %all-gather.33.cloned.1.call-start = ((), (), s32[]{:S(2)}) async-start(), calls=%async_computation.14 | async-start | bytes 5283840 | tf_op jit(solution)/shard_map/all_gather | solution.py:124
  786.4 35.0 %copy-start.3 = (f32[1032,256]{1,0:T(8,128)S(1)}, f32[1032,256]{1,0:T(8,128)}, u32[]{:S(2)}) copy-start(f32[1032,256]{1,0:T(8,128)} %copy.151) | copy-start | bytes 3170308
  786.4 71.1 %all-gather.21.cloned.1.call-start = ((), (), s32[]{:S(2)}) async-start(), calls=%async_computation.8 | async-start | bytes 5283840 | tf_op jit(solution)/shard_map/all_gather | solution.py:116
  787.0 315.6 %all-reduce.21.cloned.1.call-start = ((), (), s32[]{:S(2)}) async-start(), calls=%async_computation.24 | async-start | bytes 16908288
  947.3 155.3 %copy-start.41 = (f32[8,1,128]{2,1,0:T(1,128)S(1)}, f32[8,1,128]{2,1,0:T(1,128)}, u32[]{:S(2)}) copy-start(f32[8,1,128]{2,1,0:T(1,128)} %copy-done.40) | copy-start | bytes 12292
  947.3 161.7 %copy-start.4 = (f32[1032,684]{0,1:T(8,128)S(1)}, f32[1032,684]{0,1:T(8,128)}, u32[]{:S(2)}) copy-start(f32[1032,684]{0,1:T(8,128)} %get-tuple-element.426) | copy-start | bytes 8470660
  947.4 316.5 %all-reduce.19.cloned.1.call-start = ((), (), s32[]{:S(2)}) async-start(), calls=%async_computation.23 | async-start | bytes 180224 | tf_op jit(solution)/shard_map/psum | solution.py:502
  948.5 160.4 %copy-start.42 = (f32[2736]{0:T(1024)}, f32[2736]{0:T(1024)S(1)}, u32[]{:S(2)}) copy-start(f32[2736]{0:T(1024)S(1)} %dynamic_update_slice.51) | copy-start | bytes 32836
  948.8 160.1 %copy-start.43 = (f32[2736]{0:T(1024)}, f32[2736]{0:T(1024)S(1)}, u32[]{:S(2)}) copy-start(f32[2736]{0:T(1024)S(1)} %dynamic_update_slice.48) | copy-start | bytes 32836
  949.1 159.8 %copy-start.44 = (f32[2736]{0:T(1024)}, f32[2736]{0:T(1024)S(1)}, u32[]{:S(2)}) copy-start(f32[2736]{0:T(1024)S(1)} %dynamic_update_slice.49) | copy-start | bytes 32836
  949.4 159.5 %copy-start.45 = (f32[2736]{0:T(1024)}, f32[2736]{0:T(1024)S(1)}, u32[]{:S(2)}) copy-start(f32[2736]{0:T(1024)S(1)} %dynamic_update_slice.50) | copy-start | bytes 32836
  951.1 157.7 %copy-start.49 = (f32[1024]{0:T(1024)}, f32[1024]{0:T(1024)S(1)}, u32[]{:S(2)}) copy-start(f32[1024]{0:T(1024)S(1)} %dynamic_update_slice.44) | copy-start | bytes 12292
  951.4 157.5 %copy-start.50 = (f32[1024]{0:T(1024)}, f32[1024]{0:T(1024)S(1)}, u32[]{:S(2)}) copy-start(f32[1024]{0:T(1024)S(1)} %dynamic_update_slice.45) | copy-start | bytes 12292
  951.6 157.3 %copy-start.51 = (f32[1024]{0:T(1024)}, f32[1024]{0:T(1024)S(1)}, u32[]{:S(2)}) copy-start(f32[1024]{0:T(1024)S(1)} %dynamic_update_slice.46) | copy-start | bytes 12292
  951.8 157.1 %copy-start.48 = (f32[1024]{0:T(1024)}, f32[1024]{0:T(1024)S(1)}, u32[]{:S(2)}) copy-start(f32[1024]{0:T(1024)S(1)} %dynamic_update_slice.47) | copy-start | bytes 12292
  1109.0 172.9 %reduce-scatter.20.cloned.1.call-start = ((), (), s32[]{:S(2)}) async-start(), calls=%async_computation.21 | async-start | bytes 3170304 | tf_op jit(solution)/shard_map/reduce_scatter | solution.py:434
  1114.9 167.0 %reduce-scatter.16.cloned.1.call-start = ((), (), s32[]{:S(2)}) async-start(), calls=%async_computation.19 | async-start | bytes 3170304 | tf_op jit(solution)/shard_map/reduce_scatter | solution.py:432
  1121.4 222.8 %reduce-scatter.18.cloned.1.call-start = ((), (), s32[]{:S(2)}) async-start(), calls=%async_computation.20 | async-start | bytes 3170304 | tf_op jit(solution)/shard_map/reduce_scatter | solution.py:433
  1126.7 284.4 %reduce-scatter.14.cloned.1.call-start = ((), (), s32[]{:S(2)}) async-start(), calls=%async_computation.18 | async-start | bytes 1179648 | tf_op jit(solution)/shard_map/reduce_scatter | solution.py:487
  1132.6 345.2 %reduce-scatter.10.cloned.1.call-start = ((), (), s32[]{:S(2)}) async-start(), calls=%async_computation.16 | async-start | bytes 1179648 | tf_op jit(solution)/shard_map/reduce_scatter | solution.py:485
  1134.9 409.5 %reduce-scatter.8.cloned.1.call-start = ((), (), s32[]{:S(2)}) async-start(), calls=%async_computation.15 | async-start | bytes 1179648 | tf_op jit(solution)/shard_map/reduce_scatter | solution.py:484
  1136.9 474.2 %reduce-scatter.12.cloned.1.call-start = ((), (), s32[]{:S(2)}) async-start(), calls=%async_computation.17 | async-start | bytes 1179648 | tf_op jit(solution)/shard_map/reduce_scatter | solution.py:486
  1140.0 20.7 %copy-start.8 = (f32[1,258,1024]{2,0,1:T(1,128)S(1)}, f32[1,258,1024]{2,0,1:T(1,128)}, u32[]{:S(2)}) copy-start(f32[1,258,1024]{2,0,1:T(1,128)} %copy-done.7) | copy-start | bytes 3170308
  (49 other events, 208.7 us)
Sparse Core Ops, SparseCore 0:
  54.5 33.2 all-gather.18
  316.4 106.7 all-reduce.16
  611.6 152.3 all-reduce.22
  786.5 34.7 all-gather.32
  822.8 34.6 all-gather.20
  1109.1 154.7 all-reduce.18
Sparse Core Ops, SparseCore 1:
  318.9 40.9 all-gather.26
  361.3 42.7 all-gather.30
  430.6 34.6 all-gather.28
  467.4 42.7 all-gather.22
  512.2 41.0 all-gather.24
  947.4 155.1 all-reduce.20
  1114.9 74.5 reduce-scatter.19
  1193.5 72.6 reduce-scatter.15
  1270.2 74.1 reduce-scatter.17
  1348.3 62.7 reduce-scatter.13
  1415.3 62.5 reduce-scatter.9
  1481.9 62.5 reduce-scatter.7
  1548.7 62.4 reduce-scatter.11
where the time goes:
time: 1630 us; the launch traced here: 1620 us
  waiting for transfers between devices  928 us (57%)
  blocking collectives  336 us (21%)
  matrix products  142 us (9%)
  local copies, waits for them, and re-layouts  115 us (7%)
  other arithmetic  77.8 us (5%)
  between operations  18.3 us (1%)
    unnamed x22, waiting for transfers between devices  357 us
    psum x1, waiting for transfers between devices, local(): lax.psum((first_gain_grad, first_bias_grad, place_piece(query_bias_grad,...  94.8 us
    reduce_scatter x1, waiting for transfers between devices, local(): lax.psum_scatter(key_weight_grad, 'dp', scatter_dimension=0, tiled=True)  66.8 us
    reduce_scatter x1, waiting for transfers between devices, local(): lax.psum_scatter(output_weight_grad, 'dp', scatter_dimension=1, tiled=True)  66.8 us
    reduce_scatter x1, waiting for transfers between devices, local(): lax.psum_scatter(value_weight_grad, 'dp', scatter_dimension=0, tiled=True)  66.7 us
    reduce_scatter x1, waiting for transfers between devices, local(): lax.psum_scatter(query_weight_grad, 'dp', scatter_dimension=0, tiled=True)  66.6 us
    reduce_scatter x1, waiting for transfers between devices, local(): lax.psum_scatter(up_weight_grad, 'dp', scatter_dimension=0, tiled=True)  62.4 us
    all_gather x1, waiting for transfers between devices, feedforward_set(): lax.all_gather(gate_weight, 'dp', axis=0, tiled=True)  40.5 us
  transfers between devices with their start and end apart: 19, of which 14 were waited for; matrix products, arithmetic and copies ran while one was open for 7% of the time, Pallas kernels for 0%

commit v1 on v0

v1 whole, which is shorter than its diff:
```python
import math

import jax
import jax.numpy as jnp
from jax import lax
from jax.sharding import PartitionSpec as P

HD = 64
EPSILON = 1e-06
BF = jnp.bfloat16
F32 = jnp.float32


def swap(value, axis, offset):
    count = lax.axis_size(axis)
    return lax.ppermute(value, axis, [(i, i ^ offset) for i in range(count)])


def tensor_gather(block):
    core = swap(block, "tensor", 1)
    far = swap(block, "tensor", 2)
    diagonal = swap(far, "tensor", 1)
    return [block, core, far, diagonal]


def tensor_scatter(parts):
    core = [swap(parts[k].astype(BF), "tensor", 1) for k in (3, 1)]
    to_far = (parts[2].astype(F32) + core[0].astype(F32)).astype(BF)
    far = swap(to_far, "tensor", 2)
    return parts[0].astype(F32) + core[1].astype(F32) + far.astype(F32)


def tensor_sum(value):
    blocks = value.reshape(value.shape[0], 4, -1)
    total = blocks
    for k in (1, 2, 3):
        other = swap(blocks, "tensor", k)
        total = total + jnp.stack([other[:, r ^ k] for r in range(4)], axis=1)
    return total.reshape(value.shape)


def dp_gather(block):
    count = lax.axis_size("dp")
    column = [block] + [swap(block, "dp", 2 * k) for k in range(1, count // 2)]
    across = [swap(one, "dp", 1) for one in column]
    return [one for pair in zip(column, across) for one in pair]


def dp_order(chunks):
    stacked = jnp.stack(chunks) if isinstance(chunks, list) else chunks
    me = lax.axis_index("dp")
    count = stacked.shape[0]
    return jnp.stack([lax.dynamic_index_in_dim(stacked, me ^ r, 0, False) for r in range(count)])


def dp_scatter(chunks):
    count = chunks.shape[0]
    pairs = chunks.reshape((count // 2, 2) + chunks.shape[1:])
    across = swap(pairs[:, 1], "dp", 1)
    halves = pairs[:, 0].astype(F32) + across.astype(F32)
    total = halves[0]
    for k in range(1, count // 2):
        total = total + swap(halves[k].astype(BF), "dp", 2 * k).astype(F32)
    return total


def stats(values):
    center = jnp.mean(values, axis=-1, keepdims=True)
    spread = jnp.mean(values * values, axis=-1, keepdims=True) - center * center
    return center, lax.rsqrt(spread + EPSILON)


def normalize_back(grad_hat, unit_hat, inverse):
    return inverse * (
        grad_hat
        - jnp.mean(grad_hat, axis=-1, keepdims=True)
        - unit_hat * jnp.mean(grad_hat * unit_hat, axis=-1, keepdims=True)
    )


def mm(a, b):
    return jnp.einsum("ij,jk->ik", a, b, preferred_element_type=F32)


def mm_nt(a, b):
    return jnp.einsum("ij,kj->ik", a, b, preferred_element_type=F32)


def mm_tn(a, b):
    return jnp.einsum("ji,jk->ik", a, b, preferred_element_type=F32)


def rotary(patch_row, patch_column, place):
    quarter = HD // 4
    indices = jnp.arange(quarter).astype(F32)
    frequency = jnp.power(F32(10000.0), -indices / quarter)
    row_part = patch_row.astype(F32)[:, None] * frequency
    column_part = patch_column.astype(F32)[:, None] * frequency
    angles = 0.5 * jnp.concatenate([row_part, column_part], axis=-1)
    angles = jnp.where((place > 0)[:, None], angles, 0.0)
    return jnp.cos(angles), jnp.sin(angles)


def turn(values, cosine, sine):
    paired = values.reshape(values.shape[0], -1, HD // 2, 2)
    even, odd = paired[..., 0], paired[..., 1]
    c, s = cosine[:, None, :], sine[:, None, :]
    return jnp.stack([even * c - odd * s, even * s + odd * c], axis=-1).reshape(values.shape)


def attend(element):
    query, key, value, keep = element
    scale = 1.0 / math.sqrt(HD)
    scores = jnp.where(keep[None, :], mm_nt(query, key) * scale, -1e30)
    row_max = jnp.max(scores, axis=-1, keepdims=True)
    terms = jnp.exp(scores - row_max)
    denominator = jnp.sum(terms, axis=-1, keepdims=True)
    attended = mm((terms / denominator).astype(BF), value)
    return attended, (row_max + jnp.log(denominator))[:, 0]


def attend_back(element):
    query, key, value, keep, logsum, grad = element
    scale = 1.0 / math.sqrt(HD)
    scores = jnp.where(keep[None, :], mm_nt(query, key) * scale, -1e30)
    probs = jnp.exp(scores - logsum[:, None])
    grad_value = mm_tn(probs.astype(BF), grad)
    grad_probs = mm_nt(grad, value)
    grad_scores = (
        probs * (grad_probs - jnp.sum(probs * grad_probs, axis=-1, keepdims=True))
    ).astype(BF)
    return mm(grad_scores, key) * scale, mm_tn(grad_scores, query) * scale, grad_value


def heads(values):
    return values.reshape(values.shape[0], -1, HD).transpose(1, 0, 2)


def unheads(items):
    return items.transpose(1, 0, 2).reshape(items.shape[1], -1)


def local(
    layer_input, query_weight, key_weight, value_weight, query_bias, value_bias, first_gain, first_bias,
    mixer_gain, mixer_bias, output_weight, output_bias, second_gain, second_bias, gate_weight, up_weight,
    gate_bias, up_bias, inner_gain, inner_bias, down_weight, down_bias, cotangent, key_valid, patch_row, patch_column,
):
    ranks = lax.axis_size("tensor")
    me_t, me_d, count_d = lax.axis_index("tensor"), lax.axis_index("dp"), lax.axis_size("dp")
    width = layer_input.shape[2]
    block = layer_input.shape[1]
    padded = -(-block // 16) * 16
    head_width = query_weight.shape[1]
    hidden = gate_weight.shape[1]

    def pad(rows):
        return jnp.pad(rows, ((0, padded - block), (0, 0)))

    def cut(rows):
        return [rows[k * padded : k * padded + block] for k in range(ranks)]

    x_own = layer_input[0]
    cot_own = cotangent[0]
    small = jnp.stack(
        [query_bias, value_bias, first_gain, first_bias, mixer_gain, mixer_bias, output_bias, second_gain,
         second_bias, down_bias]
    )
    rows = jnp.concatenate([query_weight, key_weight, value_weight], axis=1)
    x_all = jnp.concatenate([pad(b) for b in tensor_gather(x_own)]).astype(F32)
    small_all = dp_order(dp_gather(small)).transpose(1, 0, 2).reshape(-1, width)
    qkv_full = dp_order(dp_gather(rows)).reshape(width, -1)
    cot_all = jnp.concatenate([pad(b) for b in tensor_gather(cot_own)])
    out_full = dp_order(dp_gather(output_weight)).transpose(1, 0, 2).reshape(head_width, width)
    gate_full = dp_order(dp_gather(gate_weight)).reshape(width, hidden)
    up_full = dp_order(dp_gather(up_weight)).reshape(width, hidden)
    down_full = dp_order(dp_gather(down_weight)).transpose(1, 0, 2).reshape(hidden, width)
    vec = small_all.astype(F32)
    own = [lax.dynamic_slice_in_dim(vec[k], me_t * head_width, head_width) for k in range(10)]
    q_bias, v_bias, m_gain, m_bias = own[0], own[1], own[4], own[5]
    f_gain, f_bias, o_bias, s_gain, s_bias, d_bias = vec[2], vec[3], vec[6], vec[7], vec[8], vec[9]
    gate_b, up_b, i_gain, i_bias = (v.astype(F32) for v in (gate_bias, up_bias, inner_gain, inner_bias))

    def tokens(vector):
        blocks = vector.reshape(ranks, block)
        picked = [jnp.pad(lax.dynamic_index_in_dim(blocks, me_t ^ r, 0, False), (0, padded - block)) for r in range(ranks)]
        return jnp.concatenate(picked)

    keep = tokens(key_valid[0]) == 1
    place = tokens(jnp.arange(ranks * block))
    cosine, sine = rotary(tokens(patch_row[0]), tokens(patch_column[0]), place)

    center, inverse_one = stats(x_all)
    unit_one = (x_all - center) * inverse_one
    first = (unit_one * f_gain + f_bias).astype(BF)
    qkv = mm(first, qkv_full)
    queries = turn(qkv[:, :head_width] + q_bias, cosine, sine).astype(BF)
    keys = turn(qkv[:, head_width : 2 * head_width], cosine, sine).astype(BF)
    values = (qkv[:, 2 * head_width :] + v_bias).astype(BF)
    queries, keys, values = heads(queries), heads(keys), heads(values)
    keeps = jnp.broadcast_to(keep, (queries.shape[0], keep.shape[0]))
    items, logsum = lax.map(attend, (queries, keys, values, keeps))
    attended = unheads(items)
    sums = tensor_sum(jnp.stack([jnp.sum(attended, -1), jnp.sum(attended * attended, -1)]))
    mean = (sums[0] / width)[:, None]
    inverse_mix = lax.rsqrt((sums[1] / width)[:, None] - mean * mean + EPSILON)
    unit_mix = (attended - mean) * inverse_mix
    mixed = (unit_mix * m_gain + m_bias).astype(BF)
    hidden_state = x_own.astype(F32) + tensor_scatter(cut(mm(mixed, out_full).astype(BF))) + o_bias

    center, inverse_two = stats(hidden_state)
    unit_two = (hidden_state - center) * inverse_two
    second_own = (unit_two * s_gain + s_bias).astype(BF)
    second = jnp.concatenate([pad(b) for b in tensor_gather(second_own)])
    gate = mm(second, gate_full) + gate_b
    up = mm(second, up_full) + up_b
    sigmoid = jax.nn.sigmoid(gate)
    activated = gate * sigmoid * up
    grad_inner = mm_nt(cot_all, down_full)
    grad_hat = grad_inner * i_gain
    sums = tensor_sum(
        jnp.stack(
            [jnp.sum(activated, -1), jnp.sum(activated * activated, -1), jnp.sum(grad_hat, -1),
             jnp.sum(grad_hat * activated, -1)]
        )
    )
    hidden_all = hidden * ranks
    mean = (sums[0] / hidden_all)[:, None]
    inverse = lax.rsqrt((sums[1] / hidden_all)[:, None] - mean * mean + EPSILON)
    unit = (activated - mean) * inverse
    inner = (unit * i_gain + i_bias).astype(BF)
    grad_mean = (sums[2] / hidden_all)[:, None]
    cross = inverse * ((sums[3] / hidden_all)[:, None] - mean * grad_mean)
    grad_activated = inverse * (grad_hat - grad_mean - unit * cross)
    grad_gate = (grad_activated * up * sigmoid * (1.0 + gate * (1.0 - sigmoid))).astype(BF)
    grad_up = (grad_activated * gate * sigmoid).astype(BF)
    grad_second = tensor_scatter(cut((mm_nt(grad_gate, gate_full) + mm_nt(grad_up, up_full)).astype(BF)))
    layer_output = (hidden_state + tensor_scatter(cut(mm(inner, down_full).astype(BF))) + d_bias).astype(BF)

    def row_chunks(grad):
        return dp_order(grad.astype(BF).reshape(count_d, width // count_d, -1))

    def column_chunks(grad):
        return dp_order(grad.astype(BF).reshape(grad.shape[0], count_d, -1).transpose(1, 0, 2))

    down_grad = dp_scatter(column_chunks(mm_tn(inner, cot_all)))
    gate_grad = dp_scatter(row_chunks(mm_tn(second, grad_gate)))
    up_grad = dp_scatter(row_chunks(mm_tn(second, grad_up)))

    cot_f = cot_own.astype(F32)
    grad_hidden = cot_f + normalize_back(grad_second * s_gain, unit_two, inverse_two)
    branch_own = grad_hidden.astype(BF)
    branch = jnp.concatenate([pad(b) for b in tensor_gather(branch_own)])
    grad_mixed = mm_nt(branch, out_full)
    grad_hat = grad_mixed * m_gain
    sums = tensor_sum(jnp.stack([jnp.sum(grad_hat, -1), jnp.sum(grad_hat * unit_mix, -1)]))
    grad_attended = (
        inverse_mix * (grad_hat - (sums[0] / width)[:, None] - unit_mix * (sums[1] / width)[:, None])
    ).astype(BF)
    out_grad = dp_scatter(column_chunks(mm_tn(mixed, branch)))
    grad_q, grad_k, grad_v = lax.map(attend_back, (queries, keys, values, keeps, logsum, heads(grad_attended)))
    grad_q = turn(unheads(grad_q), cosine, -sine).astype(BF)
    grad_k = turn(unheads(grad_k), cosine, -sine).astype(BF)
    grad_v = unheads(grad_v).astype(BF)
    grad_qkv = jnp.concatenate([grad_q, grad_k, grad_v], axis=1)
    grad_first_part = mm_nt(grad_qkv, qkv_full)
    grad_first = tensor_scatter(cut(grad_first_part.astype(BF)))
    qkv_grad = dp_scatter(row_chunks(mm_tn(first, grad_qkv)))
    input_grad = grad_hidden + normalize_back(grad_first * f_gain, unit_one[:block], inverse_one[:block])

    def total(rows):
        return jnp.sum(rows.astype(F32), axis=0)

    def place_piece(piece):
        return lax.dynamic_update_slice_in_dim(jnp.zeros((width,), F32), piece, me_t * head_width, 0)

    model = jnp.stack(
        [total(grad_first_part * unit_one), total(grad_first_part), place_piece(total(grad_q)), place_piece(total(grad_v)),
         place_piece(total(grad_mixed * unit_mix)), place_piece(total(grad_mixed)), total(branch_own),
         total(grad_second * unit_two), total(grad_second), total(cot_f)]
    )
    ffn = jnp.stack([total(grad_gate), total(grad_up), total(grad_inner * unit), total(grad_inner)])
    model = lax.psum(model, ("dp", "tensor"))
    ffn = lax.psum(ffn, "dp")
    mine = lax.dynamic_slice_in_dim(model, me_d * (width // count_d), width // count_d, 1)
    return (
        layer_output[None], input_grad[None],
        qkv_grad[:, :head_width], qkv_grad[:, head_width : 2 * head_width], qkv_grad[:, 2 * head_width :],
        mine[2], mine[3], mine[0], mine[1], mine[4], mine[5], out_grad, mine[6], mine[7], mine[8],
        gate_grad, up_grad, ffn[0], ffn[1], ffn[2], ffn[3], down_grad, mine[9],
    )


def solution(mesh):
    rows, across, tokens = P("dp", "tensor"), P("tensor", "dp"), P("dp", "tensor", None)
    model, ffn, image = P("dp"), P("tensor"), P("dp", None)
    in_specs = (
        tokens, rows, rows, rows, model, model, model, model, model, model, across, model, model, model, rows, rows,
        ffn, ffn, ffn, ffn, across, model, tokens, image, image, image,
    )
    out_specs = (
        tokens, tokens, rows, rows, rows, model, model, model, model, model, model, across, model, model, model,
        rows, rows, ffn, ffn, ffn, ffn, across, model,
    )
    return jax.shard_map(local, mesh=mesh, in_specs=in_specs, out_specs=out_specs, check_vma=False)
```

time: 1630 us -> 656 us (0.40)
  waiting for transfers between devices: 928 us -> 190 us
  blocking collectives: 336 us -> 87.9 us
  starting transfers between devices: 1.47 us -> 94.6 us
  matrix products: 142 us -> 93.7 us
    unnamed x22 -> x0, waiting for transfers between devices: 357 us -> none
    reduce_scatter x7 -> x0, waiting for transfers between devices: 329 us -> none  [the longest x1 66.8 us: local(): lax.psum_scatter(key_weight_grad, 'dp', scatter_dimension=0, tiled=True)]
    all_gather x14 -> x0, blocking collectives: 302 us -> none  [the longest x1 31.8 us: attention_set(): lax.all_gather(key_weight, 'dp', axis=0, tiled=True)]
    ppermute x0 -> x95, waiting for transfers between devices: none -> 190 us  [swap(): return lax.ppermute(value, axis, [(i, i ^ offset) for i in range(count)])]
    all_gather x8 -> x0, waiting for transfers between devices: 147 us -> none  [the longest x1 40.5 us: feedforward_set(): lax.all_gather(gate_weight, 'dp', axis=0, tiled=True)]
    psum x1 -> x0, waiting for transfers between devices: 94.8 us -> none  [local(): lax.psum((first_gain_grad, first_bias_grad, place_piece(query_bias_grad,...]
    ppermute x0 -> x95, starting transfers between devices: none -> 94.6 us  [swap(): return lax.ppermute(value, axis, [(i, i ^ offset) for i in range(count)])]
    psum x4 -> x2, blocking collectives: 34.1 us -> 87.9 us  [the longest x1 44.5 us: local(): model = lax.psum(model, ('dp', 'tensor'))]
  transfers between devices with their start and end apart: 19 -> 95, of which waited for: 14 -> 37; matrix products, arithmetic and copies ran while one was open for 7% -> 34% of each run, Pallas kernels for 0% -> 0%
where the time goes in v1:
time: 656 us; the launch traced here: 648 us
  waiting for transfers between devices  190 us (29%)
  local copies, waits for them, and re-layouts  115 us (18%)
  starting transfers between devices  94.6 us (14%)
  matrix products  93.7 us (14%)
  blocking collectives  87.9 us (13%)
  other arithmetic  63.2 us (10%)
    ppermute x95, waiting for transfers between devices, swap(): return lax.ppermute(value, axis, [(i, i ^ offset) for i in range(count)])  190 us
    ppermute x95, starting transfers between devices, swap(): return lax.ppermute(value, axis, [(i, i ^ offset) for i in range(count)])  94.6 us
    unnamed x319, local copies, waits for them, and re-layouts  45.9 us
    psum x1, blocking collectives, local(): model = lax.psum(model, ('dp', 'tensor'))  44.5 us
    psum x1, blocking collectives, local(): ffn = lax.psum(ffn, 'dp')  43.4 us
    dot_general x17, matrix products, mm_nt(): return jnp.einsum('ij,kj->ik', a, b, preferred_element_type=F32)  37.8 us
    dot_general x13, matrix products, mm(): return jnp.einsum('ij,jk->ik', a, b, preferred_element_type=F32)  30.6 us
    dot_general x13, matrix products, mm_tn(): return jnp.einsum('ji,jk->ik', a, b, preferred_element_type=F32)  25.3 us
  transfers between devices with their start and end apart: 95, of which 37 were waited for; matrix products, arithmetic and copies ran while one was open for 34% of the time, Pallas kernels for 0%

profile of v1, /device:TPU:0, one launch (start us, length us, event | category | flops | bytes accessed | tf_op | source)
XLA Modules:
  0.0 648.5 jit_solution(16600861178195443048)
XLA Ops:
  3.4 2.9 collective-permute-start.3
  34.7 3.5 collective-permute-start.13
  53.9 2.9 collective-permute-done.23
  59.9 3.3 collective-permute-done.25
  71.1 5.7 collective-permute-done.33
  77.5 5.8 collective-permute-done.34
  85.4 3.8 collective-permute-done.40
  89.8 4.8 collective-permute-done.41
  96.0 4.2 collective-permute-done.50
  101.0 5.0 collective-permute-done.51
  106.0 3.0 collective-permute-start.36
  114.3 5.1 collective-permute-done.35
  119.5 7.2 %collective-permute-done.37 = bf16[128,684]{0,1:T(8,128)(2,1)S(1)} collective-permute-done((bf16[128,684]{0,1:T(8,128)(2,1)S(1)}, bf16[128,684]{0,1:T(8,128)(2,1)S(1)}, u32[]{:S(2)}, u32[]{:S(2)}) %collective-permute-start.37) | collective-permute-done | bytes 175136 | tf_op jit(solution)/shard_map/ppermute | solution.py:16
  126.7 5.4 collective-permute-done.42
  132.6 8.9 %collective-permute-done.43 = bf16[128,684]{0,1:T(8,128)(2,1)S(1)} collective-permute-done((bf16[128,684]{0,1:T(8,128)(2,1)S(1)}, bf16[128,684]{0,1:T(8,128)(2,1)S(1)}, u32[]{:S(2)}, u32[]{:S(2)}) %collective-permute-start.43) | collective-permute-done | bytes 175136 | tf_op jit(solution)/shard_map/ppermute | solution.py:16
  143.6 6.6 %collective-permute-done.38 = bf16[128,684]{0,1:T(8,128)(2,1)S(1)} collective-permute-done((bf16[128,684]{0,1:T(8,128)(2,1)S(1)}, bf16[128,684]{0,1:T(8,128)(2,1)S(1)}, u32[]{:S(2)}, u32[]{:S(2)}) %collective-permute-start.38) | collective-permute-done | bytes 175136 | tf_op jit(solution)/shard_map/ppermute | solution.py:16
  152.7 4.5 collective-permute-done.44
  158.0 6.5 %collective-permute-done.45 = bf16[128,684]{0,1:T(8,128)(2,1)S(1)} collective-permute-done((bf16[128,684]{0,1:T(8,128)(2,1)S(1)}, bf16[128,684]{0,1:T(8,128)(2,1)S(1)}, u32[]{:S(2)}, u32[]{:S(2)}) %collective-permute-start.45) | collective-permute-done | bytes 175136 | tf_op jit(solution)/shard_map/ppermute | solution.py:16
  166.3 4.9 collective-permute-done.39
  173.5 5.0 collective-permute-done.46
  187.2 3.1 collective-permute-done.14
  192.0 3.9 collective-permute-done.16
  206.7 3.9 subtract_convert_fusion.1
  217.9 27.4 %while.26 = (s32[]{:T(128)}, f32[4,1088,64]{1,2,0:T(8,128)S(1)}, f32[4,1088]{1,0:T(4,128)S(1)}, pred[4,1088]{1,0:T(4,128)(4,1)S(1)}, bf16[4,1088,64]{2,1,0:T(8,1...) while((s32[]{:T(128)}, f32[4,1088,64]{1,2,0:T(8,128)S(1)}, ...), condition=%wide.region_5.6_spmd, body=%wide.region_2.5_spmd.sunk | while | flops 312507328 | bytes 34620160 | solution.py:201
  221.2 3.4 fusion.208
  228.0 3.4 fusion.208
  234.7 3.4 fusion.208
  241.5 3.4 fusion.208
  252.8 3.3 collective-permute-done.18
  270.1 8.5 %collective-permute-done.29 = bf16[258,1024]{1,0:T(8,128)(2,1)S(1)} collective-permute-done((bf16[258,1024]{1,0:T(8,128)(2,1)S(1)}, bf16[258,1024]{1,0:T(8,128)(2,1)S(1)}, u32[]{:S(2)}, u32[]{:S(2)}) %collective-permute-start.29) | collective-permute-done | bytes 528416 | tf_op jit(solution)/shard_map/ppermute | solution.py:16
  280.1 13.1 %collective-permute-done.31 = bf16[258,1024]{1,0:T(8,128)(2,1)S(1)} collective-permute-done((bf16[258,1024]{1,0:T(8,128)(2,1)S(1)}, bf16[258,1024]{1,0:T(8,128)(2,1)S(1)}, u32[]{:S(2)}, u32[]{:S(2)}) %collective-permute-start.31) | collective-permute-done | bytes 528416 | tf_op jit(solution)/shard_map/ppermute | solution.py:16
  299.4 7.7 %multiply_reduce_fusion.3 = (f32[1088]{0:T(1024)S(1)}, f32[1088]{0:T(1024)S(1)}, f32[1088]{0:T(1024)S(1)}, f32[1088]{0:T(1024)S(1)}, f32[1088,684]{0,1:T(8,128)}, /*index=5*/f32[1088,684]{0,1:T(8,128)}) fusion(f32[684]{0:T(1024)S(1)} %convert_element_type.434, f32[1088,684]{0,1:T(8,128)S(1)} %convolution_add_fusion.1, ...), kind=kOutput, calls=%fused_computation.93 | convolution fusion | flops 1555313664 | bytes 15441584 | tf_op jit(solution)/shard_map/ij,kj->ik/dot_general | solution.py:86
  315.9 4.6 convolution_convert_fusion.1
  320.6 4.1 convolution_convert_fusion.3
  325.2 2.9 constant_dynamic-slice_fusion.1
  332.6 3.9 multiply_reduce_fusion.2
  339.6 2.9 constant_dynamic-slice_fusion.9
  361.7 43.4 %psum.15 = f32[4,684]{1,0:T(4,128)S(1)} all-reduce(f32[4,684]{1,0:T(4,128)S(1)} %pad_maximum_fusion.6), channel_id=1, replica_groups=mesh['dp'=8,'tensor'=4] {'dp'}, use_global_device_ids=true, to_apply=%region_38.39 | all-reduce | flops 2736 | bytes 21888 | tf_op jit(solution)/shard_map/psum | solution.py:283
  413.2 22.0 %collective-permute-done.65 = bf16[258,1024]{1,0:T(8,128)(2,1)S(1)} collective-permute-done((bf16[258,1024]{1,0:T(8,128)(2,1)S(1)}, bf16[258,1024]{1,0:T(8,128)(2,1)S(1)}, u32[]{:S(2)}, u32[]{:S(2)}) %collective-permute-start.65) | collective-permute-done | bytes 528416 | tf_op jit(solution)/shard_map/ppermute | solution.py:16
  441.1 4.2 convert_reduce_fusion.6
  450.6 7.2 %collective-permute-done.67 = bf16[258,1024]{1,0:T(8,128)(2,1)S(1)} collective-permute-done((bf16[258,1024]{1,0:T(8,128)(2,1)S(1)}, bf16[258,1024]{1,0:T(8,128)(2,1)S(1)}, u32[]{:S(2)}, u32[]{:S(2)}) %collective-permute-start.67) | collective-permute-done | bytes 528416 | tf_op jit(solution)/shard_map/ppermute | solution.py:16
  466.4 11.4 %collective-permute-done.85 = bf16[128,684]{0,1:T(8,128)(2,1)S(1)} collective-permute-done((bf16[128,684]{0,1:T(8,128)(2,1)S(1)}, bf16[128,684]{0,1:T(8,128)(2,1)S(1)}, u32[]{:S(2)}, u32[]{:S(2)}) %collective-permute-start.85) | collective-permute-done | bytes 175136 | tf_op jit(solution)/shard_map/ppermute | solution.py:16
  497.3 30.6 %while.27 = (s32[]{:T(128)}, f32[4,1088,64]{1,2,0:T(8,128)}, f32[4,1088,64]{1,2,0:T(8,128)}, bf16[4,1088,64]{1,2,0:T(8,128)(2,1)S(1)}, pred[4,1088]{1,0:T(4,128)...) while((s32[]{:T(128)}, f32[4,1088,64]{1,2,0:T(8,128)}, ...), condition=%wide.region_20.21_spmd, body=%wide.region_18.20_spmd.sunk | while | flops 768388032 | bytes 38955252 | solution.py:260
  540.3 7.8 %fusion.146 = (f32[1024]{0:T(1024)}, f32[1024]{0:T(1024)}, bf16[1088,1024]{1,0:T(8,128)(2,1)S(1)}, f32[1088,1024]{1,0:T(8,128)}) fusion(f32[1088]{0:T(1024)S(1)} %copy-done.68, f32[1088]{0:T(1024)S(1)} %copy-done.75, bf16[1088,1024]{1,0:T(8,128)(2,1)} %copy-done.16, bf16[1024,768]{1,0:T(8,128)(2,1)} %bitcast.603, bf16[1088,256]{0,1:T(8,128)(2,1)S(1)} %bitcast.557, ...), kind=kOutput, calls=%fused_computation.539 | convolution fusion | flops 1724086272 | bytes 12173824 | tf_op jit(solution)/shard_map/ij,kj->ik/dot_general | solution.py:86
  548.2 4.1 convolution_convert_fusion.2
  568.9 44.5 %psum.14 = f32[10,1024]{1,0:T(8,128)} all-reduce(f32[10,1024]{1,0:T(8,128)} %stack.559), channel_id=1, replica_groups=mesh['dp'=8,'tensor'=4] {'dp','tensor'}, use_global_device_ids=true, to_apply=%region_33.34 | all-reduce | flops 10240 | bytes 81920 | tf_op jit(solution)/shard_map/psum | solution.py:282
  631.1 3.8 collective-permute-done.76
  635.0 6.8 %collective-permute-done.77 = bf16[128,768]{1,0:T(8,128)(2,1)S(1)} collective-permute-done((bf16[128,768]{1,0:T(8,128)(2,1)S(1)}, bf16[128,768]{1,0:T(8,128)(2,1)S(1)}, u32[]{:S(2)}, u32[]{:S(2)}) %collective-permute-start.77) | collective-permute-done | bytes 196640 | tf_op jit(solution)/shard_map/ppermute | solution.py:16
  (761 shorter events, 313.6 us)
Async XLA Ops:
  3.4 27.6 %collective-permute-start.3 = (bf16[10,128]{1,0:T(8,128)(2,1)}, bf16[10,128]{1,0:T(8,128)(2,1)}, u32[]{:S(2)}, u32[]{:S(2)}) collective-permute-start(bf16[10,128]{1,0:T(8,128)(2,1)} %stack.462), channel_id=1, source_target_pairs={{0,4},{4,0},{8,12},{12,8},{16,20},{20,16},{24,28},{28,24},{1,5},{5... | collective-permute-start | bytes 7688 | tf_op jit(solution)/shard_map/ppermute | solution.py:16
  6.3 25.6 %collective-permute-start.4 = (bf16[10,128]{1,0:T(8,128)(2,1)}, bf16[10,128]{1,0:T(8,128)(2,1)}, u32[]{:S(2)}, u32[]{:S(2)}) collective-permute-start(bf16[10,128]{1,0:T(8,128)(2,1)} %stack.462), channel_id=1, source_target_pairs={{0,8},{4,12},{8,0},{12,4},{16,24},{20,28},{24,16},{28,20},{1,9},{5... | collective-permute-start | bytes 7688 | tf_op jit(solution)/shard_map/ppermute | solution.py:16
  7.9 26.9 %collective-permute-start.6 = (bf16[10,128]{1,0:T(8,128)(2,1)}, bf16[10,128]{1,0:T(8,128)(2,1)}, u32[]{:S(2)}, u32[]{:S(2)}) collective-permute-start(bf16[10,128]{1,0:T(8,128)(2,1)} %stack.462), channel_id=1, source_target_pairs={{0,16},{4,20},{8,24},{12,28},{16,0},{20,4},{24,8},{28,12},{1,17},{... | collective-permute-start | bytes 7688 | tf_op jit(solution)/shard_map/ppermute | solution.py:16
  10.5 29.0 %collective-permute-start.8 = (bf16[10,128]{1,0:T(8,128)(2,1)}, bf16[10,128]{1,0:T(8,128)(2,1)}, u32[]{:S(2)}, u32[]{:S(2)}) collective-permute-start(bf16[10,128]{1,0:T(8,128)(2,1)} %stack.462), channel_id=1, source_target_pairs={{0,24},{4,28},{8,16},{12,20},{16,8},{20,12},{24,0},{28,4},{1,25},{... | collective-permute-start | bytes 7688 | tf_op jit(solution)/shard_map/ppermute | solution.py:16
  15.1 94.9 %collective-permute-start.10 = (bf16[128,768]{1,0:T(8,128)(2,1)}, bf16[128,768]{1,0:T(8,128)(2,1)}, u32[]{:S(2)}, u32[]{:S(2)}) collective-permute-start(bf16[128,768]{1,0:T(8,128)(2,1)} %constant_dynamic-update-slice_fusion.16), channel_id=1, source_target_pairs={{0,4},{4,0},{8,12},{12,8},{16,20},{20,16},{24,28},{28,24},{1,5},{5... | collective-permute-start | bytes 589832 | tf_op jit(solution)/shard_map/ppermute | solution.py:16
  31.0 82.1 %collective-permute-start.11 = (bf16[128,768]{1,0:T(8,128)(2,1)}, bf16[128,768]{1,0:T(8,128)(2,1)}, u32[]{:S(2)}, u32[]{:S(2)}) collective-permute-start(bf16[128,768]{1,0:T(8,128)(2,1)} %constant_dynamic-update-slice_fusion.16), channel_id=1, source_target_pairs={{0,8},{4,12},{8,0},{12,4},{16,24},{20,28},{24,16},{28,20},{1,9},{5... | collective-permute-start | bytes 589832 | tf_op jit(solution)/shard_map/ppermute | solution.py:16
  34.7 146.8 %collective-permute-start.13 = (bf16[128,768]{1,0:T(8,128)(2,1)}, bf16[128,768]{1,0:T(8,128)(2,1)}, u32[]{:S(2)}, u32[]{:S(2)}) collective-permute-start(bf16[128,768]{1,0:T(8,128)(2,1)} %constant_dynamic-update-slice_fusion.16), channel_id=1, source_target_pairs={{0,16},{4,20},{8,24},{12,28},{16,0},{20,4},{24,8},{28,12},{1,17},{... | collective-permute-start | bytes 589832 | tf_op jit(solution)/shard_map/ppermute | solution.py:16
  39.5 10.2 %collective-permute-start.20 = (bf16[256,128]{0,1:T(8,128)(2,1)}, bf16[256,128]{0,1:T(8,128)(2,1)}, u32[]{:S(2)}, u32[]{:S(2)}) collective-permute-start(bf16[256,128]{0,1:T(8,128)(2,1)} %copy-done.53), channel_id=1, source_target_pairs={{0,4},{4,0},{8,12},{12,8},{16,20},{20,16},{24,28},{28,24},{1,5},{5... | collective-permute-start | bytes 196616 | tf_op jit(solution)/shard_map/ppermute | solution.py:16
  63.2 123.8 %collective-permute-start.15 = (bf16[128,768]{1,0:T(8,128)(2,1)}, bf16[128,768]{1,0:T(8,128)(2,1)S(1)}, u32[]{:S(2)}, u32[]{:S(2)}) collective-permute-start(bf16[128,768]{1,0:T(8,128)(2,1)} %constant_dynamic-update-slice_fusion.16), channel_id=1, source_target_pairs={{0,24},{4,28},{8,16},{12,20},{16,8},{20,12},{24,0},{28,4},{1,25},{... | collective-permute-start | bytes 589832 | tf_op jit(solution)/shard_map/ppermute | solution.py:16
  110.0 86.0 %collective-permute-start.1 = (bf16[258,1024]{1,0:T(8,128)(2,1)S(1)}, bf16[258,1024]{1,0:T(8,128)(2,1)S(1)}, u32[]{:S(2)}, u32[]{:S(2)}) collective-permute-start(bf16[258,1024]{1,0:T(8,128)(2,1)S(1)} %bitcast.562), channel_id=1, source_target_pairs={{0,2},{1,3},{2,0},{3,1},{4,6},{5,7},{6,4},{7,5},{8,10},{9,11},{10,... | collective-permute-start | bytes 1585160 | tf_op jit(solution)/shard_map/ppermute | solution.py:16
  114.3 83.8 %collective-permute-start = (bf16[258,1024]{1,0:T(8,128)(2,1)S(1)}, bf16[258,1024]{1,0:T(8,128)(2,1)S(1)}, u32[]{:S(2)}, u32[]{:S(2)}) collective-permute-start(bf16[258,1024]{1,0:T(8,128)(2,1)S(1)} %bitcast.563), channel_id=1, source_target_pairs={{0,1},{1,0},{2,3},{3,2},{4,5},{5,4},{6,7},{7,6},{8,9},{9,8},{10,11... | collective-permute-start | bytes 1585160 | tf_op jit(solution)/shard_map/ppermute | solution.py:16
  181.5 14.8 %collective-permute-start.53 = (bf16[684,128]{1,0:T(8,128)(2,1)}, bf16[684,128]{1,0:T(8,128)(2,1)}, u32[]{:S(2)}, u32[]{:S(2)}) collective-permute-start(bf16[684,128]{1,0:T(8,128)(2,1)} %param.50), channel_id=1, source_target_pairs={{0,16},{4,20},{8,24},{12,28},{16,0},{20,4},{24,8},{28,12},{1,17},{... | collective-permute-start | bytes 525320 | tf_op jit(solution)/shard_map/ppermute | solution.py:16
  187.1 79.2 %collective-permute-start.55 = (bf16[684,128]{1,0:T(8,128)(2,1)}, bf16[684,128]{1,0:T(8,128)(2,1)}, u32[]{:S(2)}, u32[]{:S(2)}) collective-permute-start(bf16[684,128]{1,0:T(8,128)(2,1)} %param.50), channel_id=1, source_target_pairs={{0,24},{4,28},{8,16},{12,20},{16,8},{20,12},{24,0},{28,4},{1,25},{... | collective-permute-start | bytes 525320 | tf_op jit(solution)/shard_map/ppermute | solution.py:16
  195.9 98.4 %collective-permute-start.48 = (bf16[258,1024]{1,0:T(8,128)(2,1)}, bf16[258,1024]{1,0:T(8,128)(2,1)}, u32[]{:S(2)}, u32[]{:S(2)}) collective-permute-start(bf16[258,1024]{1,0:T(8,128)(2,1)} %bitcast.85), channel_id=1, source_target_pairs={{0,2},{1,3},{2,0},{3,1},{4,6},{5,7},{6,4},{7,5},{8,10},{9,11},{10,... | collective-permute-start | bytes 1585160 | tf_op jit(solution)/shard_map/ppermute | solution.py:16
  196.3 65.4 %collective-permute-start.52 = (bf16[684,128]{1,0:T(8,128)(2,1)}, bf16[684,128]{1,0:T(8,128)(2,1)}, u32[]{:S(2)}, u32[]{:S(2)}) collective-permute-start(bf16[684,128]{1,0:T(8,128)(2,1)} %collective-permute-done.51), channel_id=1, source_target_pairs={{0,4},{4,0},{8,12},{12,8},{16,20},{20,16},{24,28},{28,24},{1,5},{5... | collective-permute-start | bytes 525320 | tf_op jit(solution)/shard_map/ppermute | solution.py:16
  198.1 68.3 %collective-permute-start.54 = (bf16[684,128]{1,0:T(8,128)(2,1)}, bf16[684,128]{1,0:T(8,128)(2,1)}, u32[]{:S(2)}, u32[]{:S(2)}) collective-permute-start(bf16[684,128]{1,0:T(8,128)(2,1)} %collective-permute-done.53), channel_id=1, source_target_pairs={{0,4},{4,0},{8,12},{12,8},{16,20},{20,16},{24,28},{28,24},{1,5},{5... | collective-permute-start | bytes 525320 | tf_op jit(solution)/shard_map/ppermute | solution.py:16
  264.0 14.6 %collective-permute-start.29 = (bf16[258,1024]{1,0:T(8,128)(2,1)S(1)}, bf16[258,1024]{1,0:T(8,128)(2,1)S(1)}, u32[]{:S(2)}, u32[]{:S(2)}) collective-permute-start(bf16[258,1024]{1,0:T(8,128)(2,1)S(1)} %add_convert_fusion.8), channel_id=1, source_target_pairs={{0,2},{1,3},{2,0},{3,1},{4,6},{5,7},{6,4},{7,5},{8,10},{9,11},{10,... | collective-permute-start | bytes 1585160 | tf_op jit(solution)/shard_map/ppermute | solution.py:16
  266.3 33.0 %collective-permute-start.47 = (bf16[258,1024]{1,0:T(8,128)(2,1)}, bf16[258,1024]{1,0:T(8,128)(2,1)S(1)}, u32[]{:S(2)}, u32[]{:S(2)}) collective-permute-start(bf16[258,1024]{1,0:T(8,128)(2,1)} %bitcast.85), channel_id=1, source_target_pairs={{0,1},{1,0},{2,3},{3,2},{4,5},{5,4},{6,7},{7,6},{8,9},{9,8},{10,11... | collective-permute-start | bytes 1585160 | tf_op jit(solution)/shard_map/ppermute | solution.py:16
  266.5 13.4 %collective-permute-start.56 = (bf16[684,128]{1,0:T(8,128)(2,1)}, bf16[684,128]{1,0:T(8,128)(2,1)S(1)}, u32[]{:S(2)}, u32[]{:S(2)}) collective-permute-start(bf16[684,128]{1,0:T(8,128)(2,1)} %collective-permute-done.55), channel_id=1, source_target_pairs={{0,4},{4,0},{8,12},{12,8},{16,20},{20,16},{24,28},{28,24},{1,5},{5... | collective-permute-start | bytes 525320 | tf_op jit(solution)/shard_map/ppermute | solution.py:16
  279.4 13.8 %collective-permute-start.31 = (bf16[258,1024]{1,0:T(8,128)(2,1)S(1)}, bf16[258,1024]{1,0:T(8,128)(2,1)S(1)}, u32[]{:S(2)}, u32[]{:S(2)}) collective-permute-start(bf16[258,1024]{1,0:T(8,128)(2,1)S(1)} %add_convert_fusion.7), channel_id=1, source_target_pairs={{0,2},{1,3},{2,0},{3,1},{4,6},{5,7},{6,4},{7,5},{8,10},{9,11},{10,... | collective-permute-start | bytes 1585160 | tf_op jit(solution)/shard_map/ppermute | solution.py:16
  280.1 14.8 %collective-permute-start.30 = (bf16[258,1024]{1,0:T(8,128)(2,1)S(1)}, bf16[258,1024]{1,0:T(8,128)(2,1)S(1)}, u32[]{:S(2)}, u32[]{:S(2)}) collective-permute-start(bf16[258,1024]{1,0:T(8,128)(2,1)S(1)} %add_convert_fusion.7), channel_id=1, source_target_pairs={{0,1},{1,0},{2,3},{3,2},{4,5},{5,4},{6,7},{7,6},{8,9},{9,8},{10,11... | collective-permute-start | bytes 1585160 | tf_op jit(solution)/shard_map/ppermute | solution.py:16
  330.8 78.4 %collective-permute-start.91 = (bf16[4,684,128]{2,0,1:T(4,128)(2,1)}, bf16[4,684,128]{2,0,1:T(4,128)(2,1)S(1)}, u32[]{:S(2)}, u32[]{:S(2)}) collective-permute-start(bf16[4,684,128]{2,0,1:T(4,128)(2,1)} %copy.181), channel_id=1, source_target_pairs={{0,4},{4,0},{8,12},{12,8},{16,20},{20,16},{24,28},{28,24},{1,5},{5... | collective-permute-start | bytes 2101256 | tf_op jit(solution)/shard_map/ppermute | solution.py:16
  345.1 66.0 %collective-permute-start.87 = (bf16[4,128,684]{1,0,2:T(4,128)(2,1)}, bf16[4,128,684]{1,0,2:T(4,128)(2,1)}, u32[]{:S(2)}, u32[]{:S(2)}) collective-permute-start(bf16[4,128,684]{1,0,2:T(4,128)(2,1)} %copy.171), channel_id=1, source_target_pairs={{0,4},{4,0},{8,12},{12,8},{16,20},{20,16},{24,28},{28,24},{1,5},{5... | collective-permute-start | bytes 2101256 | tf_op jit(solution)/shard_map/ppermute | solution.py:16
  354.8 51.0 %collective-permute-start.61 = (bf16[258,1024]{1,0:T(8,128)(2,1)}, bf16[258,1024]{1,0:T(8,128)(2,1)}, u32[]{:S(2)}, u32[]{:S(2)}) collective-permute-start(bf16[258,1024]{1,0:T(8,128)(2,1)} %get-tuple-element.339), channel_id=1, source_target_pairs={{0,1},{1,0},{2,3},{3,2},{4,5},{5,4},{6,7},{7,6},{8,9},{9,8},{10,11... | collective-permute-start | bytes 1585160 | tf_op jit(solution)/shard_map/ppermute | solution.py:16
  358.5 48.8 %collective-permute-start.64 = (bf16[258,1024]{1,0:T(8,128)(2,1)}, bf16[258,1024]{1,0:T(8,128)(2,1)}, u32[]{:S(2)}, u32[]{:S(2)}) collective-permute-start(bf16[258,1024]{1,0:T(8,128)(2,1)} %get-tuple-element.337), channel_id=1, source_target_pairs={{0,1},{1,0},{2,3},{3,2},{4,5},{5,4},{6,7},{7,6},{8,9},{9,8},{10,11... | collective-permute-start | bytes 1585160 | tf_op jit(solution)/shard_map/ppermute | solution.py:16
  360.6 84.6 %collective-permute-start.83 = (bf16[4,128,684]{1,0,2:T(4,128)(2,1)}, bf16[4,128,684]{1,0,2:T(4,128)(2,1)}, u32[]{:S(2)}, u32[]{:S(2)}) collective-permute-start(bf16[4,128,684]{1,0,2:T(4,128)(2,1)} %copy.161), channel_id=1, source_target_pairs={{0,4},{4,0},{8,12},{12,8},{16,20},{20,16},{24,28},{28,24},{1,5},{5... | collective-permute-start | bytes 2101256 | tf_op jit(solution)/shard_map/ppermute | solution.py:16
  405.8 31.7 %collective-permute-start.60 = (bf16[258,1024]{1,0:T(8,128)(2,1)}, bf16[258,1024]{1,0:T(8,128)(2,1)S(1)}, u32[]{:S(2)}, u32[]{:S(2)}) collective-permute-start(bf16[258,1024]{1,0:T(8,128)(2,1)} %get-tuple-element.338), channel_id=1, source_target_pairs={{0,1},{1,0},{2,3},{3,2},{4,5},{5,4},{6,7},{7,6},{8,9},{9,8},{10,11... | collective-permute-start | bytes 1585160 | tf_op jit(solution)/shard_map/ppermute | solution.py:16
  409.2 29.5 %collective-permute-start.62 = (bf16[258,1024]{1,0:T(8,128)(2,1)S(1)}, bf16[258,1024]{1,0:T(8,128)(2,1)S(1)}, u32[]{:S(2)}, u32[]{:S(2)}) collective-permute-start(bf16[258,1024]{1,0:T(8,128)(2,1)S(1)} %add_convert_fusion.6), channel_id=1, source_target_pairs={{0,2},{1,3},{2,0},{3,1},{4,6},{5,7},{6,4},{7,5},{8,10},{9,11},{10,... | collective-permute-start | bytes 1585160 | tf_op jit(solution)/shard_map/ppermute | solution.py:16
  411.1 24.1 %collective-permute-start.65 = (bf16[258,1024]{1,0:T(8,128)(2,1)S(1)}, bf16[258,1024]{1,0:T(8,128)(2,1)S(1)}, u32[]{:S(2)}, u32[]{:S(2)}) collective-permute-start(bf16[258,1024]{1,0:T(8,128)(2,1)S(1)} %add_convert_fusion.4), channel_id=1, source_target_pairs={{0,2},{1,3},{2,0},{3,1},{4,6},{5,7},{6,4},{7,5},{8,10},{9,11},{10,... | collective-permute-start | bytes 1585160 | tf_op jit(solution)/shard_map/ppermute | solution.py:16
  413.1 35.0 %collective-permute-start.92 = (bf16[684,128]{1,0:T(8,128)(2,1)S(1)}, bf16[684,128]{1,0:T(8,128)(2,1)S(1)}, u32[]{:S(2)}, u32[]{:S(2)}) collective-permute-start(bf16[684,128]{1,0:T(8,128)(2,1)S(1)} %get-tuple-element.386), channel_id=1, source_target_pairs={{0,8},{4,12},{8,0},{12,4},{16,24},{20,28},{24,16},{28,20},{1,9},{5... | collective-permute-start | bytes 525320 | tf_op jit(solution)/shard_map/ppermute | solution.py:16
  435.2 13.9 %collective-permute-start.93 = (bf16[684,128]{1,0:T(8,128)(2,1)S(1)}, bf16[684,128]{1,0:T(8,128)(2,1)S(1)}, u32[]{:S(2)}, u32[]{:S(2)}) collective-permute-start(bf16[684,128]{1,0:T(8,128)(2,1)S(1)} %get-tuple-element.388), channel_id=1, source_target_pairs={{0,16},{4,20},{8,24},{12,28},{16,0},{20,4},{24,8},{28,12},{1,17},{... | collective-permute-start | bytes 525320 | tf_op jit(solution)/shard_map/ppermute | solution.py:16
  437.5 13.1 %collective-permute-start.94 = (bf16[684,128]{1,0:T(8,128)(2,1)S(1)}, bf16[684,128]{1,0:T(8,128)(2,1)S(1)}, u32[]{:S(2)}, u32[]{:S(2)}) collective-permute-start(bf16[684,128]{1,0:T(8,128)(2,1)S(1)} %get-tuple-element.387), channel_id=1, source_target_pairs={{0,24},{4,28},{8,16},{12,20},{16,8},{20,12},{24,0},{28,4},{1,25},{... | collective-permute-start | bytes 525320 | tf_op jit(solution)/shard_map/ppermute | solution.py:16
  438.7 20.0 %collective-permute-start.88 = (bf16[128,684]{0,1:T(8,128)(2,1)S(1)}, bf16[128,684]{0,1:T(8,128)(2,1)S(1)}, u32[]{:S(2)}, u32[]{:S(2)}) collective-permute-start(bf16[128,684]{0,1:T(8,128)(2,1)S(1)} %get-tuple-element.389), channel_id=1, source_target_pairs={{0,8},{4,12},{8,0},{12,4},{16,24},{20,28},{24,16},{28,20},{1,9},{5... | collective-permute-start | bytes 525320 | tf_op jit(solution)/shard_map/ppermute | solution.py:16
  445.2 12.6 %collective-permute-start.67 = (bf16[258,1024]{1,0:T(8,128)(2,1)S(1)}, bf16[258,1024]{1,0:T(8,128)(2,1)S(1)}, u32[]{:S(2)}, u32[]{:S(2)}) collective-permute-start(bf16[258,1024]{1,0:T(8,128)(2,1)S(1)} %get-tuple-element.304), channel_id=1, source_target_pairs={{0,2},{1,3},{2,0},{3,1},{4,6},{5,7},{6,4},{7,5},{8,10},{9,11},{10,... | collective-permute-start | bytes 1585160 | tf_op jit(solution)/shard_map/ppermute | solution.py:16
  448.1 14.6 %collective-permute-start.89 = (bf16[128,684]{0,1:T(8,128)(2,1)S(1)}, bf16[128,684]{0,1:T(8,128)(2,1)S(1)}, u32[]{:S(2)}, u32[]{:S(2)}) collective-permute-start(bf16[128,684]{0,1:T(8,128)(2,1)S(1)} %get-tuple-element.391), channel_id=1, source_target_pairs={{0,16},{4,20},{8,24},{12,28},{16,0},{20,4},{24,8},{28,12},{1,17},{... | collective-permute-start | bytes 525320 | tf_op jit(solution)/shard_map/ppermute | solution.py:16
  449.1 13.6 %collective-permute-start.90 = (bf16[128,684]{0,1:T(8,128)(2,1)S(1)}, bf16[128,684]{0,1:T(8,128)(2,1)S(1)}, u32[]{:S(2)}, u32[]{:S(2)}) collective-permute-start(bf16[128,684]{0,1:T(8,128)(2,1)S(1)} %get-tuple-element.390), channel_id=1, source_target_pairs={{0,24},{4,28},{8,16},{12,20},{16,8},{20,12},{24,0},{28,4},{1,25},{... | collective-permute-start | bytes 525320 | tf_op jit(solution)/shard_map/ppermute | solution.py:16
  450.6 28.0 %collective-permute-start.66 = (bf16[258,1024]{1,0:T(8,128)(2,1)S(1)}, bf16[258,1024]{1,0:T(8,128)(2,1)S(1)}, u32[]{:S(2)}, u32[]{:S(2)}) collective-permute-start(bf16[258,1024]{1,0:T(8,128)(2,1)S(1)} %get-tuple-element.304), channel_id=1, source_target_pairs={{0,1},{1,0},{2,3},{3,2},{4,5},{5,4},{6,7},{7,6},{8,9},{9,8},{10,11... | collective-permute-start | bytes 1585160 | tf_op jit(solution)/shard_map/ppermute | solution.py:16
  457.8 20.8 %collective-permute-start.68 = (bf16[258,1024]{1,0:T(8,128)(2,1)S(1)}, bf16[258,1024]{1,0:T(8,128)(2,1)S(1)}, u32[]{:S(2)}, u32[]{:S(2)}) collective-permute-start(bf16[258,1024]{1,0:T(8,128)(2,1)S(1)} %collective-permute-done.67), channel_id=1, source_target_pairs={{0,1},{1,0},{2,3},{3,2},{4,5},{5,4},{6,7},{7,6},{8,9},{9,8},{10,11... | collective-permute-start | bytes 1585160 | tf_op jit(solution)/shard_map/ppermute | solution.py:16
  462.7 15.1 %collective-permute-start.85 = (bf16[128,684]{0,1:T(8,128)(2,1)S(1)}, bf16[128,684]{0,1:T(8,128)(2,1)S(1)}, u32[]{:S(2)}, u32[]{:S(2)}) collective-permute-start(bf16[128,684]{0,1:T(8,128)(2,1)S(1)} %get-tuple-element.394), channel_id=1, source_target_pairs={{0,16},{4,20},{8,24},{12,28},{16,0},{20,4},{24,8},{28,12},{1,17},{... | collective-permute-start | bytes 525320 | tf_op jit(solution)/shard_map/ppermute | solution.py:16
  462.7 15.1 %collective-permute-start.86 = (bf16[128,684]{0,1:T(8,128)(2,1)S(1)}, bf16[128,684]{0,1:T(8,128)(2,1)S(1)}, u32[]{:S(2)}, u32[]{:S(2)}) collective-permute-start(bf16[128,684]{0,1:T(8,128)(2,1)S(1)} %get-tuple-element.393), channel_id=1, source_target_pairs={{0,24},{4,28},{8,16},{12,20},{16,8},{20,12},{24,0},{28,4},{1,25},{... | collective-permute-start | bytes 525320 | tf_op jit(solution)/shard_map/ppermute | solution.py:16
  490.2 124.8 %collective-permute-start.79 = (bf16[4,256,128]{2,1,0:T(8,128)(2,1)}, bf16[4,256,128]{2,1,0:T(8,128)(2,1)}, u32[]{:S(2)}, u32[]{:S(2)}) collective-permute-start(bf16[4,256,128]{2,1,0:T(8,128)(2,1)} %slice_bitcast_fusion.14), channel_id=1, source_target_pairs={{0,4},{4,0},{8,12},{12,8},{16,20},{20,16},{24,28},{28,24},{1,5},{5... | collective-permute-start | bytes 786440 | tf_op jit(solution)/shard_map/ppermute | solution.py:16
  558.3 63.9 %collective-permute-start.75 = (bf16[4,128,768]{2,1,0:T(8,128)(2,1)S(1)}, bf16[4,128,768]{2,1,0:T(8,128)(2,1)}, u32[]{:S(2)}, u32[]{:S(2)}) collective-permute-start(bf16[4,128,768]{2,1,0:T(8,128)(2,1)S(1)} %slice_bitcast_fusion.2), channel_id=1, source_target_pairs={{0,4},{4,0},{8,12},{12,8},{16,20},{20,16},{24,28},{28,24},{1,5},{5... | collective-permute-start | bytes 2359304 | tf_op jit(solution)/shard_map/ppermute | solution.py:16
  561.4 58.0 %collective-permute-start.73 = (bf16[258,1024]{1,0:T(8,128)(2,1)}, bf16[258,1024]{1,0:T(8,128)(2,1)}, u32[]{:S(2)}, u32[]{:S(2)}) collective-permute-start(bf16[258,1024]{1,0:T(8,128)(2,1)} %get-tuple-element.335), channel_id=1, source_target_pairs={{0,1},{1,0},{2,3},{3,2},{4,5},{5,4},{6,7},{7,6},{8,9},{9,8},{10,11... | collective-permute-start | bytes 1585160 | tf_op jit(solution)/shard_map/ppermute | solution.py:16
  561.4 81.2 %collective-permute-start.72 = (bf16[258,1024]{1,0:T(8,128)(2,1)}, bf16[258,1024]{1,0:T(8,128)(2,1)S(1)}, u32[]{:S(2)}, u32[]{:S(2)}) collective-permute-start(bf16[258,1024]{1,0:T(8,128)(2,1)} %get-tuple-element.334), channel_id=1, source_target_pairs={{0,1},{1,0},{2,3},{3,2},{4,5},{5,4},{6,7},{7,6},{8,9},{9,8},{10,11... | collective-permute-start | bytes 1585160 | tf_op jit(solution)/shard_map/ppermute | solution.py:16
  616.3 9.7 %collective-permute-start.80 = (bf16[256,128]{1,0:T(8,128)(2,1)S(1)}, bf16[256,128]{1,0:T(8,128)(2,1)S(1)}, u32[]{:S(2)}, u32[]{:S(2)}) collective-permute-start(bf16[256,128]{1,0:T(8,128)(2,1)S(1)} %get-tuple-element.409), channel_id=1, source_target_pairs={{0,8},{4,12},{8,0},{12,4},{16,24},{20,28},{24,16},{28,20},{1,9},{5... | collective-permute-start | bytes 196616 | tf_op jit(solution)/shard_map/ppermute | solution.py:16
  622.2 20.4 %collective-permute-start.74 = (bf16[258,1024]{1,0:T(8,128)(2,1)S(1)}, bf16[258,1024]{1,0:T(8,128)(2,1)S(1)}, u32[]{:S(2)}, u32[]{:S(2)}) collective-permute-start(bf16[258,1024]{1,0:T(8,128)(2,1)S(1)} %add_convert_fusion.3), channel_id=1, source_target_pairs={{0,2},{1,3},{2,0},{3,1},{4,6},{5,7},{6,4},{7,5},{8,10},{9,11},{10,... | collective-permute-start | bytes 1585160 | tf_op jit(solution)/shard_map/ppermute | solution.py:16
  627.1 14.7 %collective-permute-start.77 = (bf16[128,768]{1,0:T(8,128)(2,1)S(1)}, bf16[128,768]{1,0:T(8,128)(2,1)S(1)}, u32[]{:S(2)}, u32[]{:S(2)}) collective-permute-start(bf16[128,768]{1,0:T(8,128)(2,1)S(1)} %get-tuple-element.385), channel_id=1, source_target_pairs={{0,16},{4,20},{8,24},{12,28},{16,0},{20,4},{24,8},{28,12},{1,17},{... | collective-permute-start | bytes 589832 | tf_op jit(solution)/shard_map/ppermute | solution.py:16
  628.9 12.9 %collective-permute-start.78 = (bf16[128,768]{1,0:T(8,128)(2,1)S(1)}, bf16[128,768]{1,0:T(8,128)(2,1)S(1)}, u32[]{:S(2)}, u32[]{:S(2)}) collective-permute-start(bf16[128,768]{1,0:T(8,128)(2,1)S(1)} %get-tuple-element.384), channel_id=1, source_target_pairs={{0,24},{4,28},{8,16},{12,20},{16,8},{20,12},{24,0},{28,4},{1,25},{... | collective-permute-start | bytes 589832 | tf_op jit(solution)/shard_map/ppermute | solution.py:16
  (142 other events, 1309.2 us)
